TPU v7x, 1024 devices: a whole 4x8x16 slice. The times are simulated.
1024 devices in a mesh: space: 256 (over z, y, core), mem: 4 (over x).
Axes of the slice: x: 4, y: 8, z: 16, core: 2. Of those that a mesh axis runs over, the one named last changes fastest.
Arguments:
- member_heat_solute: float32 [128, 2, 4096, 128], P('mem', None, 'space'), may hold values from -6 to 6
- velocity: float32 [128, 4096, 128], P('mem', 'space'), may hold values from 0.2 to 0.6
- phase_mask: int32 [4096, 128], P('space'), may hold values 0 or 1
- obs_index: int32 [4096], P('space'), may hold values from 0 to 2047
- obs_value: float32 [4096], P('space'), may hold values from -6 to 6
- obs_error: float32 [4096], P('space'), may hold values from 0.3 to 3
Outputs:
- analysis_hc: float32 [128, 2, 4096, 128], P('mem', None, 'space')
- analysis_velocity: float32 [128, 4096, 128], P('mem', 'space')
Inputs may be any that keep to these rules, and one draw needn't show every extreme that they name: `obs_index`: observation o lies in slab o // 16; its entry counts cells row by row inside that slab.
All inputs are finite; a program needn't handle non-finite values. No bound on the sum of `phase_mask` on one device may be relied on, other than what follows from the above.
Results may differ from a plain program's by a relative error of at most 0.00015.
Values sent between devices are 32-bit elements; how exact they have to be, the bound alone decides.
No kernel may reach another device: no remote copies, remote signals or barrier semaphores. Data moves between devices by JAX's collectives and lax.ppermute only.
A program may use at most 32 MiB of HBM per device.

v0:
```python
import jax
import jax.numpy as jnp
from jax import lax
from jax.sharding import PartitionSpec as P

heat_diffusion = 0.15
advection = 0.4
solute_diffusion = 0.05
segregation = 0.3
momentum_diffusion = 0.1
darcy_drag = 0.5
mushy_ratio = 1.0 / 3.0


def with_halo(cells, sides, width):
    for axis, dim in sides:
        count = lax.axis_size(axis)
        ends = count - 1
        head = lax.slice_in_dim(cells, 0, width, axis=dim)
        tail = lax.slice_in_dim(cells, cells.shape[dim] - width, cells.shape[dim], axis=dim)
        cells = jnp.concatenate(
            [
                lax.ppermute(tail, axis, [(i, (i + 1) % count) for i in range(ends)]),
                cells,
                lax.ppermute(head, axis, [((i + 1) % count, i) for i in range(ends)]),
            ],
            axis=dim,
        )
    return cells


def lateral(field):
    left = jnp.concatenate([field[..., :1], field[..., :-1]], axis=-1)
    right = jnp.concatenate([field[..., 1:], field[..., -1:]], axis=-1)
    return left + right - 2.0 * field


def advance(padded_heat, padded_temp, padded_solute, padded_speed, mushy):
    heat = padded_heat[..., 1:-1, :]
    temp = padded_temp[..., 1:-1, :]
    solute = padded_solute[..., 1:-1, :]
    speed = padded_speed[..., 1:-1, :]
    temp_lap = padded_temp[..., 2:, :] + padded_temp[..., :-2, :] - 2.0 * temp + lateral(temp)
    solute_lap = (
        padded_solute[..., 2:, :] + padded_solute[..., :-2, :] - 2.0 * solute + lateral(solute)
    )
    speed_lap = padded_speed[..., 2:, :] + padded_speed[..., :-2, :] - 2.0 * speed + lateral(speed)
    new_heat = (
        heat + heat_diffusion * temp_lap - advection * speed * (heat - padded_heat[..., :-2, :])
    )
    new_solute = (
        solute
        + solute_diffusion * solute_lap
        - advection * speed * (solute - padded_solute[..., :-2, :])
        + segregation * mushy * (temp - solute)
    )
    new_speed = speed + momentum_diffusion * speed_lap - darcy_drag * mushy * speed
    return (new_heat, new_solute, new_speed)


def factorize(matrix):
    order = matrix.shape[0]
    positions = jnp.arange(order, dtype=jnp.int32)

    def column(j, lower):
        lower_row = lax.dynamic_slice_in_dim(lower, j, 1, 0)[0]
        matrix_col = lax.dynamic_slice_in_dim(matrix, j, 1, 1)[:, 0]
        values = matrix_col - jnp.dot(lower, lower_row, precision=lax.Precision.HIGHEST)
        pivot = jnp.sqrt(jnp.sum(jnp.where(positions == j, values, 0.0)))
        new_col = jnp.where(positions >= j, values / pivot, 0.0)
        return lax.dynamic_update_slice(lower, new_col[:, None], (jnp.int32(0), j))

    return lax.fori_loop(0, order, column, jnp.zeros((order, order), jnp.float32))


def invert_lower(lower):
    order = lower.shape[0]
    positions = jnp.arange(order, dtype=jnp.int32)

    def row_step(i, inverse):
        lower_row = lax.dynamic_slice_in_dim(lower, i, 1, 0)[0]
        pivot = jnp.sum(jnp.where(positions == i, lower_row, 0.0))
        unit = jnp.where(positions == i, 1.0, 0.0).astype(jnp.float32)
        new_row = (unit - jnp.dot(lower_row, inverse, precision=lax.Precision.HIGHEST)) / pivot
        return lax.dynamic_update_slice(inverse, new_row[None, :], (i, jnp.int32(0)))

    return lax.fori_loop(0, order, row_step, jnp.zeros((order, order), jnp.float32))


def analysis_weights(gram, project):
    members = gram.shape[0]
    ident = jnp.eye(members, dtype=jnp.float32)
    lower = factorize(ident + gram)
    lower_inverse = invert_lower(lower)
    inverse_root = lower_inverse.T
    mean_offset = jnp.dot(
        inverse_root,
        jnp.dot(lower_inverse, project, precision=lax.Precision.HIGHEST),
        precision=lax.Precision.HIGHEST,
    )
    center = ident - 1.0 / members
    combined = mean_offset[:, None] / jnp.sqrt(jnp.float32(members - 1)) + inverse_root
    return 1.0 / members + jnp.dot(center, combined, precision=lax.Precision.HIGHEST)


def on_device(member_heat_solute, velocity, phase_mask, obs_index, obs_value, obs_error):
    members = member_heat_solute.shape[0]
    mushy = phase_mask.astype(jnp.float32)
    factor = 1.0 - mushy * (1.0 - mushy_ratio)
    heat = member_heat_solute[:, 0]
    solute = member_heat_solute[:, 1]
    speed = velocity
    for section in range(2):
        field_stack = jnp.stack([heat, heat * factor, solute, speed], axis=1)
        padded = with_halo(field_stack, (("space", 2),), 1)
        heat, solute, speed = advance(padded[:, 0], padded[:, 1], padded[:, 2], padded[:, 3], mushy)
    temp = heat * factor
    flat_temp = temp.reshape(members, -1)
    cell_ids = jnp.arange(flat_temp.shape[1], dtype=jnp.int32)
    selector = jnp.where(obs_index[:, None] == cell_ids[None, :], 1.0, 0.0).astype(jnp.float32)
    observed_own = jnp.dot(flat_temp, selector.T, precision=lax.Precision.HIGHEST)
    measured_values = lax.all_gather(observed_own, "mem", axis=0, tiled=True)
    ensemble = measured_values.shape[0]
    mean_obs = jnp.mean(measured_values, axis=0)
    spread = (measured_values - mean_obs[None, :]).T / (
        obs_error[:, None] * jnp.sqrt(jnp.float32(ensemble - 1))
    )
    innovation = (obs_value - mean_obs) / obs_error
    local_gram = jnp.dot(spread.T, spread, precision=lax.Precision.HIGHEST)
    local_project = jnp.dot(spread.T, innovation, precision=lax.Precision.HIGHEST)
    gram, project = lax.psum((local_gram, local_project), "space")
    mixing = analysis_weights(gram, project)
    states = jnp.concatenate([heat[:, None], solute[:, None], speed[:, None]], axis=1)
    first_member = lax.axis_index("mem") * members
    weight_cols = lax.dynamic_slice_in_dim(mixing, first_member, members, 1)
    result = jnp.einsum(
        "kfzw,kj->jfzw",
        lax.all_gather(states, "mem", axis=0, tiled=True),
        weight_cols,
        precision=lax.Precision.HIGHEST,
    )
    return (result[:, :2], result[:, 2])


def solution(mesh):
    return jax.shard_map(
        on_device,
        mesh=mesh,
        in_specs=(
            P("mem", None, "space", None),
            P("mem", "space", None),
            P("space", None),
            P("space"),
            P("space"),
            P("space"),
        ),
        out_specs=(P("mem", None, "space", None), P("mem", "space", None)),
        check_vma=False,
    )
```

profile of v0, /device:TPU:1, one launch (start us, length us, event | category | flops | bytes accessed | tf_op | source)
XLA Modules:
  0.0 1011.4 jit_solution(16523383614169326647)
XLA Ops:
  8.8 1.1 fusion.84
  10.2 4.6 collective-permute-start
  14.8 12.8 %collective-permute-start.1 = (f32[32,4,1,128]{3,0,2,1:T(8,128)S(1)}, f32[32,4,1,128]{3,0,2,1:T(8,128)S(1)}, u32[]{:S(2)}, u32[]{:S(2)}) collective-permute-start(f32[32,4,1,128]{3,0,2,1:T(8,128)S(1)} %get-tuple-element.237), channel_id=1, source_target_pairs={{4,0},{8,4},{12,8},{16,12},{20,16},{24,20},{28,24},{32,28},{36,32}... | collective-permute-start | bytes 196616 | tf_op jit(solution)/shard_map/ppermute | solution.py:25
  27.6 0.9 collective-permute-done.1
  30.2 1.9 collective-permute-start.2
  32.1 2.4 collective-permute-start.3
  34.6 3.1 collective-permute-done.3
  39.7 9.1 all-gather
  49.0 1.0 fusion.81
  50.4 0.9 pad_maximum_fusion.2
  51.6 500.0 %psum.15 = f32[128]{0:T(128)S(1)} all-reduce(f32[128]{0:T(128)S(1)} %convolution_bitcast_fusion.5), channel_id=1, replica_groups=mesh['space'=256,'mem'=4] {'space'}, use_global_device_ids=true, to_apply=%region_8.9 | all-reduce | flops 128 | bytes 1024 | tf_op jit(solution)/shard_map/psum | solution.py:131
  551.6 0.9 convert_add_fusion
  552.5 258.7 %while.30 = (s32[]{:T(128)}, f32[128,128]{1,0:T(8,128)S(1)}, f32[128,128]{0,1:T(8,128)S(1)}, s32[]{:T(128)}, s32[]{:T(128)}) while((s32[]{:T(128)}, f32[128,128]{1,0:T(8,128)S(1)}, f32[128,128]{0,1:T(8,128)S(1)}, s32[]{:T(128)}, s32[]{:T(128)}) %tuple.105), condition=%wide.region_4.5_spmd.clone.clone, body=%wide.region_2.0_spmd.clone.clone.sunk | while | flops 197505 | bytes 71765 | solution.py:73
  552.5 0.8 fusion.115
  554.5 0.8 fusion.115
  556.5 0.8 fusion.115
  558.5 0.8 fusion.115
  560.5 0.8 fusion.115
  562.6 0.8 fusion.115
  564.6 0.8 fusion.115
  566.6 0.8 fusion.115
  568.6 0.8 fusion.115
  570.7 0.8 fusion.115
  572.7 0.8 fusion.115
  574.7 0.8 fusion.115
  576.7 0.8 fusion.115
  578.8 0.8 fusion.115
  580.8 0.8 fusion.115
  811.3 186.3 %while.29 = (s32[]{:T(128)}, f32[128,128]{1,0:T(8,128)S(1)}, f32[128,128]{1,0:T(8,128)S(1)}, s32[]{:T(128)}, s32[]{:T(128)}) while((s32[]{:T(128)}, f32[128,128]{1,0:T(8,128)S(1)}, f32[128,128]{1,0:T(8,128)S(1)}, s32[]{:T(128)}, s32[]{:T(128)}) %tuple.108), condition=%wide.region_7.8_spmd.clone, body=%wide.region_5.7_spmd.clone.sunk | while | flops 197505 | bytes 70725 | solution.py:87
  998.3 3.6 fusion.71
  1002.0 1.1 copy.31
  1003.1 0.9 copy.32
  (936 shorter events, 343.8 us)
Async XLA Ops:
  8.0 2.0 copy-start
  8.0 543.6 %all-reduce.2.cloned.1.call-start = ((), (), s32[]{:S(2)}) async-start(), calls=%async_computation | async-start | bytes 131072 | tf_op jit(solution)/shard_map/psum | solution.py:131
  10.2 17.4 %collective-permute-start = (f32[32,4,1,128]{3,0,2,1:T(8,128)S(1)}, f32[32,4,1,128]{3,0,2,1:T(8,128)S(1)}, u32[]{:S(2)}, u32[]{:S(2)}) collective-permute-start(f32[32,4,1,128]{3,0,2,1:T(8,128)S(1)} %get-tuple-element.236), channel_id=1, source_target_pairs={{0,4},{4,8},{8,12},{12,16},{16,20},{20,24},{24,28},{28,32},{32,36}... | collective-permute-start | bytes 196616 | tf_op jit(solution)/shard_map/ppermute | solution.py:23
  14.8 13.6 %collective-permute-start.1 = (f32[32,4,1,128]{3,0,2,1:T(8,128)S(1)}, f32[32,4,1,128]{3,0,2,1:T(8,128)S(1)}, u32[]{:S(2)}, u32[]{:S(2)}) collective-permute-start(f32[32,4,1,128]{3,0,2,1:T(8,128)S(1)} %get-tuple-element.237), channel_id=1, source_target_pairs={{4,0},{8,4},{12,8},{16,12},{20,16},{24,20},{28,24},{32,28},{36,32}... | collective-permute-start | bytes 196616 | tf_op jit(solution)/shard_map/ppermute | solution.py:25
  30.1 4.4 copy-start.2
  30.2 4.4 collective-permute-start.2
  32.1 5.6 collective-permute-start.3
  38.7 0.7 copy-start.1
  50.0 948.2 %all-gather.3.cloned.1.call-start = ((), (), s32[]{:S(2)}) async-start(), calls=%async_computation.1 | async-start | bytes 3932160 | tf_op jit(solution)/shard_map/all_gather | solution.py:138
  50.4 1.0 copy-start.3
Sparse Core Ops, SparseCore 0:
  50.2 325.3 all-reduce.1
Sparse Core Ops, SparseCore 1:
  551.6 46.3 all-gather.2
where the time goes:
time: 1010 us
  blocking collectives  509 us (50%)
  matrix products  213 us (21%)
  loops' own time  95.3 us (9%)
  other arithmetic  82.9 us (8%)
  local copies, waits for them, and re-layouts  69.6 us (7%)
  starting transfers between devices  21.8 us (2%)
  between operations  15.8 us (2%)
    psum x1, blocking collectives, on_device(): gram, project = lax.psum((local_gram, local_project), 'space')  500 us
    dot_general x128, matrix products, column(): jnp.dot(lower, lower_row, precision=lax.Precision.HIGHEST)  105 us
    dot_general x128, matrix products, row_step(): jnp.dot(lower_row, inverse, precision=lax.Precision.HIGHEST)  102 us
    another operation x1, loops' own time, factorize(): lax.fori_loop(0, order, column, jnp.zeros((order, order), jnp.float32))  92.6 us
    reduce_sum x128, other arithmetic, row_step(): pivot = jnp.sum(jnp.where(positions == i, lower_row, 0.0))  77.6 us
    dynamic_update_slice x128, local copies, waits for them, and re-layouts, column(): return lax.dynamic_update_slice(lower, new_col[:, None], (jnp.int32(0), j))  45.9 us
  transfers between devices with their start and end apart: 6, of which 2 were waited for; matrix products, arithmetic and copies ran while one was open for 35% of the time, Pallas kernels for 0%

commit v1 on v0

v1 whole, which is shorter than its diff:
```python
import jax
import jax.numpy as jnp
from jax import lax
from jax.experimental import pallas as pl
from jax.experimental.pallas import tpu as pltpu
from jax.sharding import Mesh
from jax.sharding import PartitionSpec as P

heat_diffusion = 0.15
advection = 0.4
solute_diffusion = 0.05
segregation = 0.3
momentum_diffusion = 0.1
darcy_drag = 0.5
mushy_ratio = 1.0 / 3.0

SPACE = ("z", "y", "core")
HIGHEST = lax.Precision.HIGHEST


def lateral(field):
    left = jnp.concatenate([field[..., :1], field[..., :-1]], axis=-1)
    right = jnp.concatenate([field[..., 1:], field[..., -1:]], axis=-1)
    return left + right - 2.0 * field


def laplacian(padded):
    centre = padded[:, 1:-1]
    return padded[:, 2:] + padded[:, :-2] - 2.0 * centre + lateral(centre)


def advance(heat, solute, speed, mushy, factor):
    temp = heat * factor
    inner_heat = heat[:, 1:-1]
    inner_solute = solute[:, 1:-1]
    inner_speed = speed[:, 1:-1]
    inner_mushy = mushy[1:-1]
    carried = advection * inner_speed
    new_heat = (
        inner_heat + heat_diffusion * laplacian(temp) - carried * (inner_heat - heat[:, :-2])
    )
    new_solute = (
        inner_solute
        + solute_diffusion * laplacian(solute)
        - carried * (inner_solute - solute[:, :-2])
        + segregation * inner_mushy * (temp[:, 1:-1] - inner_solute)
    )
    new_speed = (
        inner_speed
        + momentum_diffusion * laplacian(speed)
        - darcy_drag * inner_mushy * inner_speed
    )
    return new_heat, new_solute, new_speed


def shared(value, axes):
    count = lax.axis_size(axes)
    return lax.all_to_all(
        jnp.broadcast_to(value[None], (count,) + value.shape), axes, 0, 0
    )


def weights_kernel(gram_ref, project_ref, out_ref, left, right):
    members = gram_ref.shape[0]
    rows = lax.broadcasted_iota(jnp.int32, (members, members), 0)
    cols = lax.broadcasted_iota(jnp.int32, (members, members), 1)
    ident = jnp.where(rows == cols, 1.0, 0.0)
    left[0:members, :] = gram_ref[...] + ident
    right[0:members, :] = ident
    left[members:, :] = jnp.broadcast_to(project_ref[...], (8, members))
    right[members:, :] = jnp.zeros((8, members), jnp.float32)
    total = members + 8
    for j in range(members):
        base = (j // 8) * 8
        row_a = left[j : j + 1, :]
        row_m = right[j : j + 1, :]
        pivot = lax.rsqrt(row_a[:, j : j + 1])
        scaled_a = row_a * pivot
        scaled_m = row_m * pivot
        column = left[base:total, j : j + 1] * pivot
        position = lax.broadcasted_iota(jnp.int32, (total - base, 1), 0) + base
        column = jnp.where(position > j, column, 0.0)
        left[base:total, :] = left[base:total, :] - column * scaled_a
        right[base:total, :] = right[base:total, :] - column * scaled_m
        right[j : j + 1, :] = scaled_m
    shift = -right[members : members + 1, :]
    combined = right[0:members, :] + shift * (1.0 / (members - 1) ** 0.5)
    mean = jnp.sum(combined, axis=1, keepdims=True) * (1.0 / members)
    out_ref[...] = combined - mean + 1.0 / members


def analysis_weights(gram, project):
    members = gram.shape[0]
    return pl.pallas_call(
        weights_kernel,
        out_shape=jax.ShapeDtypeStruct((members, members), jnp.float32),
        scratch_shapes=[
            pltpu.VMEM((members + 8, members), jnp.float32),
            pltpu.VMEM((members + 8, members), jnp.float32),
        ],
    )(gram, project)


def on_device(member_heat_solute, velocity, phase_mask, obs_index, obs_value, obs_error):
    members, _, depth, width = member_heat_solute.shape
    mushy = phase_mask.astype(jnp.float32)
    fields = jnp.concatenate(
        [
            member_heat_solute[:, 0],
            member_heat_solute[:, 1],
            velocity,
            mushy[None],
        ],
        axis=0,
    )
    count = lax.axis_size(SPACE)
    position = lax.axis_index(SPACE)
    above = lax.ppermute(fields[:, -2:], SPACE, [(i, i + 1) for i in range(count - 1)])
    below = lax.ppermute(fields[:, :2], SPACE, [(i + 1, i) for i in range(count - 1)])
    padded = jnp.concatenate([above, fields, below], axis=1)
    mushy = padded[3 * members]
    factor = 1.0 - mushy * (1.0 - mushy_ratio)
    heat = padded[:members]
    solute = padded[members : 2 * members]
    speed = padded[2 * members : 3 * members]
    heat, solute, speed = advance(heat, solute, speed, mushy, factor)
    row = lax.broadcasted_iota(jnp.int32, (depth + 2, 1), 0)
    outside = ((row == 0) & (position == 0)) | ((row == depth + 1) & (position == count - 1))
    heat = jnp.where(outside, 0.0, heat)
    solute = jnp.where(outside, 0.0, solute)
    speed = jnp.where(outside, 0.0, speed)
    heat, solute, speed = advance(heat, solute, speed, mushy[1:-1], factor[1:-1])

    temp = heat * factor[2:-2]
    flat_temp = temp.reshape(members, -1)
    cell_ids = jnp.arange(flat_temp.shape[1], dtype=jnp.int32)
    selector = jnp.where(obs_index[:, None] == cell_ids[None, :], 1.0, 0.0).astype(jnp.float32)
    observed_own = jnp.dot(selector, flat_temp.T, precision=HIGHEST)
    message = jnp.concatenate([observed_own, obs_value[:, None], obs_error[:, None]], axis=1)
    arrived = shared(message, ("y", "core", "mem"))
    mem_size = lax.axis_size("mem")
    slabs = arrived.shape[0] // mem_size
    n_obs = message.shape[0]
    arrived = arrived.reshape(slabs, mem_size, n_obs, members + 2)
    ensemble = mem_size * members
    measured = arrived[..., :members].transpose(0, 2, 1, 3).reshape(slabs * n_obs, ensemble)
    value = arrived[:, 0, :, members].reshape(slabs * n_obs)
    error = arrived[:, 0, :, members + 1].reshape(slabs * n_obs)
    mean_obs = jnp.mean(measured, axis=1)
    spread = (measured - mean_obs[:, None]) / (
        error[:, None] * jnp.sqrt(jnp.float32(ensemble - 1))
    )
    innovation = (value - mean_obs) / error
    pieces = mem_size * lax.axis_size("core")
    piece = lax.axis_index("mem") * lax.axis_size("core") + lax.axis_index("core")
    height = ensemble // pieces
    own_cols = lax.dynamic_slice_in_dim(spread, piece * height, height, 1)
    left = jnp.concatenate([own_cols, innovation[:, None]], axis=1)
    part = lax.dot_general(left, spread, (((0,), (0,)), ((), ())), precision=HIGHEST)
    part = jnp.sum(shared(part, "z"), axis=0)
    project = part[height:]
    gram = shared(part[:height], ("mem", "core")).reshape(ensemble, ensemble)
    weights = analysis_weights(gram, project)

    mem_index = lax.axis_index("mem")
    weights = lax.dynamic_slice_in_dim(weights, mem_index * members, members, 0)
    states = jnp.stack([heat, solute, speed], axis=1)
    result = None
    for step in range(mem_size):
        if step:
            source = lax.ppermute(
                states, "mem", [(i, (i + step) % mem_size) for i in range(mem_size)]
            )
        else:
            source = states
        origin = (mem_index - step + mem_size) % mem_size
        block = lax.dynamic_slice_in_dim(weights, origin * members, members, 1)
        term = jnp.einsum("kfzw,jk->jfzw", source, block, precision=HIGHEST)
        result = term if result is None else result + term
    return (result[:, :2], result[:, 2])


def solution(mesh):
    shaped = Mesh(mesh.devices.reshape(16, 8, 2, 4), ("z", "y", "core", "mem"))
    return jax.shard_map(
        on_device,
        mesh=shaped,
        in_specs=(
            P("mem", None, SPACE, None),
            P("mem", SPACE, None),
            P(SPACE, None),
            P(SPACE),
            P(SPACE),
            P(SPACE),
        ),
        out_specs=(P("mem", None, SPACE, None), P("mem", SPACE, None)),
        check_vma=False,
    )
```

time: 1010 us -> 127 us (0.13)
  blocking collectives: 509 us -> 0 us
  matrix products: 213 us -> 6.9 us
  loops' own time: 95.3 us -> 0 us
  other arithmetic: 82.9 us -> 4.47 us
  local copies, waits for them, and re-layouts: 69.6 us -> 13.1 us
  starting transfers between devices: 21.8 us -> 57.3 us
  waiting for transfers between devices: 4.09 us -> 30.7 us
  between operations: 15.8 us -> 1.13 us
  Pallas kernels: 0 us -> 12.4 us
    psum x1 -> x0, blocking collectives: 500 us -> none  [on_device(): gram, project = lax.psum((local_gram, local_project), 'space')]
    dot_general x263 -> x6, matrix products: 213 us -> 6.9 us  [the longest x4 6.38 us: on_device(): term = jnp.einsum('kfzw,jk->jfzw', source, block, precision=HIGHEST)]
    another operation x2 -> x0, loops' own time: 95.3 us -> none  [the longest x1 92.6 us: factorize(): lax.fori_loop(0, order, column, jnp.zeros((order, order), jnp.float32))]
    reduce_sum x129 -> x2, other arithmetic: 77.7 us -> 0.14 us  [the longest x1 0.12 us: on_device(): mean_obs = jnp.mean(measured, axis=1)]
    dynamic_update_slice x256 -> x0, local copies, waits for them, and re-layouts: 49.9 us -> none  [the longest x128 45.9 us: column(): return lax.dynamic_update_slice(lower, new_col[:, None], (jnp.int32(0), j))]
    all_to_all x0 -> x3, waiting for transfers between devices: none -> 29.3 us  [shared(): lax.all_to_all(jnp.broadcast_to(value[None], (count,) + value.shape), axe...]
    all_to_all x0 -> x3, starting transfers between devices: none -> 28.6 us  [shared(): lax.all_to_all(jnp.broadcast_to(value[None], (count,) + value.shape), axe...]
    broadcast_in_dim x128 -> x5, local copies, waits for them, and re-layouts: 14.5 us -> 1.54 us  [the longest x3 1.37 us: shared(): jnp.broadcast_to(value[None], (count,) + value.shape)]
  transfers between devices with their start and end apart: 6 -> 8, of which waited for: 2 -> 4; matrix products, arithmetic and copies ran while one was open for 35% -> 8% of each run, Pallas kernels for 0% -> 10%
where the time goes in v1:
time: 127 us; the launch traced here: 126 us
  starting transfers between devices  57.3 us (45%)
  waiting for transfers between devices  30.7 us (24%)
  local copies, waits for them, and re-layouts  13.1 us (10%)
  Pallas kernels  12.4 us (10%)
  matrix products  6.9 us (5%)
  other arithmetic  4.47 us (4%)
    all_to_all x3, waiting for transfers between devices, shared(): lax.all_to_all(jnp.broadcast_to(value[None], (count,) + value.shape), axe...  29.3 us
    all_to_all x3, starting transfers between devices, shared(): lax.all_to_all(jnp.broadcast_to(value[None], (count,) + value.shape), axe...  28.6 us
    ppermute x1, starting transfers between devices, on_device(): lax.ppermute(fields[:, :2], SPACE, [(i + 1, i) for i in range(count - 1)])  16.1 us
    pallas_call x1, Pallas kernels, analysis_weights(): pl.pallas_call(weights_kernel, out_shape=jax.ShapeDtypeStruct((members, m...  12.4 us
    ppermute x3, starting transfers between devices, on_device(): lax.ppermute(states, 'mem', [(i, (i + step) % mem_size) for i in range(me...  10.8 us
    dot_general x4, matrix products, on_device(): term = jnp.einsum('kfzw,jk->jfzw', source, block, precision=HIGHEST)  6.38 us
    unnamed x23, local copies, waits for them, and re-layouts  5.78 us
  transfers between devices with their start and end apart: 8, of which 4 were waited for; matrix products, arithmetic and copies ran while one was open for 8% of the time, Pallas kernels for 10%

profile of v1, /device:TPU:1, one launch (start us, length us, event | category | flops | bytes accessed | tf_op | source)
XLA Modules:
  0.0 126.1 jit_solution(11584023470058259418)
XLA Ops:
  0.6 0.7 convert_element_type.3
  1.3 1.0 copy.61
  2.4 1.1 fusion.77
  3.7 16.1 %collective-permute-start.1 = (f32[97,2,128]{2,0,1:T(8,128)S(1)}, f32[97,2,128]{2,0,1:T(8,128)S(1)}, u32[]{:S(2)}, u32[]{:S(2)}) collective-permute-start(f32[97,2,128]{2,0,1:T(8,128)S(1)} %get-tuple-element.31), channel_id=1, source_target_pairs={{4,0},{8,4},{12,8},{16,12},{20,16},{24,20},{28,24},{32,28},{36,32}... | collective-permute-start | bytes 297992 | tf_op jit(solution)/shard_map/ppermute | solution.py:119
  19.7 1.9 %collective-permute-start = (f32[97,2,128]{2,0,1:T(8,128)S(1)}, f32[97,2,128]{2,0,1:T(8,128)S(1)}, u32[]{:S(2)}, u32[]{:S(2)}) collective-permute-start(f32[97,2,128]{2,0,1:T(8,128)S(1)} %get-tuple-element.32), channel_id=1, source_target_pairs={{0,4},{4,8},{8,12},{12,16},{16,20},{20,24},{24,28},{28,32},{32,36}... | collective-permute-start | bytes 297992 | tf_op jit(solution)/shard_map/ppermute | solution.py:118
  21.9 1.5 %collective-permute-done = f32[97,2,128]{2,0,1:T(8,128)S(1)} collective-permute-done((f32[97,2,128]{2,0,1:T(8,128)S(1)}, f32[97,2,128]{2,0,1:T(8,128)S(1)}, u32[]{:S(2)}, u32[]{:S(2)}) %collective-permute-start) | collective-permute-done | bytes 99360 | tf_op jit(solution)/shard_map/ppermute | solution.py:118
  23.5 0.5 copy-done.2
  27.1 0.4 slice-done
  27.5 0.5 multiply_bitcast_fusion
  28.7 1.1 reshape.103
  29.8 4.6 %all-to-all-start = ((f32[64,1,544]{2,1,0:T(1,128)}), f32[64,1,544]{2,1,0:T(1,128)S(1)}, u32[]{:S(2)}, u32[]{:S(2)}) async-start(f32[64,1,544]{2,1,0:T(1,128)} %reshape.103), calls=%async_computation | async-start | bytes 327680 | tf_op jit(solution)/shard_map/all_to_all | solution.py:58
  34.8 4.5 %collective-permute-start.4 = (f32[32,3,16,128]{3,0,2,1:T(8,128)S(1)}, f32[32,3,16,128]{3,0,2,1:T(8,128)S(1)}, u32[]{:S(2)}, u32[]{:S(2)}) collective-permute-start(f32[32,3,16,128]{3,0,2,1:T(8,128)S(1)} %pad_maximum_fusion.1), channel_id=1, source_target_pairs={{0,3},{1,0},{2,1},{3,2},{4,7},{5,4},{6,5},{7,6},{8,11},{9,8},{10,9... | collective-permute-start | bytes 2359304 | tf_op jit(solution)/shard_map/ppermute | solution.py:171
  39.3 5.6 %all-to-all-done = f32[64,1,544]{2,1,0:T(1,128)S(1)} async-done(((f32[64,1,544]{2,1,0:T(1,128)}), f32[64,1,544]{2,1,0:T(1,128)S(1)}, u32[]{:S(2)}, u32[]{:S(2)}) %all-to-all-start) | async-done | bytes 139296 | tf_op jit(solution)/shard_map/all_to_all | solution.py:58
  44.9 0.5 broadcast.90
  45.4 1.0 reduce.7
  48.7 0.7 broadcast_in_dim.74
  49.4 15.0 %all-to-all-start.1 = ((f32[16,17,128]{2,1,0:T(8,128)}), f32[16,17,128]{2,1,0:T(8,128)S(1)}, u32[]{:S(2)}, u32[]{:S(2)}) async-start(f32[16,17,128]{2,1,0:T(8,128)} %broadcast_in_dim.74), calls=%async_computation.1 | async-start | bytes 393216 | tf_op jit(solution)/shard_map/all_to_all | solution.py:58
  64.4 2.2 %collective-permute-start.2 = (f32[32,3,16,128]{3,0,2,1:T(8,128)S(1)}, f32[32,3,16,128]{3,0,2,1:T(8,128)}, u32[]{:S(2)}, u32[]{:S(2)}) collective-permute-start(f32[32,3,16,128]{3,0,2,1:T(8,128)S(1)} %pad_maximum_fusion.1), channel_id=1, source_target_pairs={{0,1},{1,2},{2,3},{3,0},{4,5},{5,6},{6,7},{7,4},{8,9},{9,10},{10,1... | collective-permute-start | bytes 2359304 | tf_op jit(solution)/shard_map/ppermute | solution.py:171
  66.6 4.1 %collective-permute-start.3 = (f32[32,3,16,128]{3,0,2,1:T(8,128)S(1)}, f32[32,3,16,128]{3,0,2,1:T(8,128)}, u32[]{:S(2)}, u32[]{:S(2)}) collective-permute-start(f32[32,3,16,128]{3,0,2,1:T(8,128)S(1)} %pad_maximum_fusion.1), channel_id=1, source_target_pairs={{0,2},{1,3},{2,0},{3,1},{4,6},{5,7},{6,4},{7,5},{8,10},{9,11},{10,... | collective-permute-start | bytes 2359304 | tf_op jit(solution)/shard_map/ppermute | solution.py:171
  70.7 6.0 %all-to-all-done.1 = f32[16,17,128]{2,1,0:T(8,128)S(1)} async-done(((f32[16,17,128]{2,1,0:T(8,128)}), f32[16,17,128]{2,1,0:T(8,128)S(1)}, u32[]{:S(2)}, u32[]{:S(2)}) %all-to-all-start.1) | async-done | bytes 139296 | tf_op jit(solution)/shard_map/all_to_all | solution.py:58
  76.8 0.6 broadcast_in_dim.75
  77.5 8.9 %all-to-all-start.2 = ((f32[8,16,128]{2,1,0:T(8,128)}), f32[8,16,128]{2,1,0:T(8,128)S(1)}, u32[]{:S(2)}, u32[]{:S(2)}) async-start(f32[8,16,128]{2,1,0:T(8,128)} %broadcast_in_dim.75), calls=%async_computation.2 | async-start | bytes 131072 | tf_op jit(solution)/shard_map/all_to_all | solution.py:58
  86.3 0.6 slice.340.project_ref
  86.9 17.6 %all-to-all-done.2 = f32[8,16,128]{2,1,0:T(8,128)S(1)} async-done(((f32[8,16,128]{2,1,0:T(8,128)}), f32[8,16,128]{2,1,0:T(8,128)S(1)}, u32[]{:S(2)}, u32[]{:S(2)}) %all-to-all-start.2) | async-done | bytes 65568 | tf_op jit(solution)/shard_map/all_to_all | solution.py:58
  104.6 0.6 copy-done.1
  105.2 12.4 %shard_map.77 = f32[128,128]{1,0:T(8,128)} custom-call(f32[128,128]{1,0:T(8,128)} %bitcast.74, f32[1,128]{1,0:T(1,128)} %slice.340.project_ref), custom_call_target="tpu_custom_call" | custom-call | tf_op jit(solution)/shard_map/pallas_call | solution.py:94
  117.6 1.6 %fusion.62 = f32[32,3,16,128]{3,0,2,1:T(8,128)S(1)} fusion(f32[128,128]{1,0:T(8,128)} %shard_map.77, s32[]{:T(128)S(6)} %select_n.66, s32[]{:T(128)S(6)} %select_n.69, f32[32,1,16,128]{3,0,2,1:T(8,128)S(1)} %get-tuple-element.39, f32[32,1,16,128]{3,0,2,1:T(8,128)S(1)} %fusion.40, f32[32,1,16,128]{3,0,2,1:T(8,128)S(1)} %bitcast.66), kind=kOutput, calls=%fused_computation.105 | convolution fusion | flops 75890688 | bytes 1589256 | tf_op jit(solution)/shard_map/kfzw,jk->jfzw/dot_general | solution.py:178
  119.2 0.8 fusion.58
  120.1 2.0 %convolution_add_fusion.1 = f32[32,3,16,128]{3,0,2,1:T(8,128)S(1)} fusion(f32[32,3,16,128]{3,0,2,1:T(8,128)S(1)} %fusion.62, f32[32,3,16,128]{3,0,2,1:T(8,128)} %collective-permute-done.2, f32[128,128]{1,0:T(8,128)S(1)} %copy-done, s32[]{:T(128)S(6)} %select_n.66, s32[]{:T(128)S(6)} %select_n.73), kind=kOutput, calls=%fused_computation.1 | convolution fusion | flops 75694080 | bytes 2375688 | tf_op jit(solution)/shard_map/kfzw,jk->jfzw/dot_general | solution.py:178
  122.0 2.0 %fusion = f32[32,3,16,128]{3,0,2,1:T(8,128)S(1)} fusion(f32[32,3,16,128]{3,0,2,1:T(8,128)S(1)} %fusion.58, f32[32,3,16,128]{3,0,2,1:T(8,128)S(1)} %convolution_add_fusion.1, f32[32,3,16,128]{3,0,2,1:T(8,128)} %collective-permute-done.3, f32[128,128]{1,0:T(8,128)S(1)} %copy-done, s32[]{:T(128)S(6)} %select_n.66, s32[]{:T(128)S(6)} %select_n.76), kind=kOutput, calls=%fused_computation.2 | convolution fusion | flops 75890688 | bytes 3162120 | tf_op jit(solution)/shard_map/kfzw,jk->jfzw/dot_general | solution.py:178
  124.1 1.1 copy.68
  125.2 0.9 copy.69
  (73 shorter events, 6.7 us)
Async XLA Ops:
  3.4 18.2 %copy-start.3 = (s32[16,128]{1,0:T(8,128)S(1)}, s32[16,128]{1,0:T(8,128)}, u32[]{:S(2)}) copy-start(s32[16,128]{1,0:T(8,128)} %param.8) | copy-start | bytes 24580
  3.5 18.3 %copy-start.5 = (f32[16]{0:T(128)S(1)}, f32[16]{0:T(128)}, u32[]{:S(2)}) copy-start(f32[16]{0:T(128)} %param.10) | copy-start | bytes 196
  3.5 18.3 %copy-start.6 = (f32[16]{0:T(128)S(1)}, f32[16]{0:T(128)}, u32[]{:S(2)}) copy-start(f32[16]{0:T(128)} %param.11) | copy-start | bytes 196
  3.7 18.2 %collective-permute-start.1 = (f32[97,2,128]{2,0,1:T(8,128)S(1)}, f32[97,2,128]{2,0,1:T(8,128)S(1)}, u32[]{:S(2)}, u32[]{:S(2)}) collective-permute-start(f32[97,2,128]{2,0,1:T(8,128)S(1)} %get-tuple-element.31), channel_id=1, source_target_pairs={{4,0},{8,4},{12,8},{16,12},{20,16},{24,20},{28,24},{32,28},{36,32}... | collective-permute-start | bytes 297992 | tf_op jit(solution)/shard_map/ppermute | solution.py:119
  19.7 3.6 %collective-permute-start = (f32[97,2,128]{2,0,1:T(8,128)S(1)}, f32[97,2,128]{2,0,1:T(8,128)S(1)}, u32[]{:S(2)}, u32[]{:S(2)}) collective-permute-start(f32[97,2,128]{2,0,1:T(8,128)S(1)} %get-tuple-element.32), channel_id=1, source_target_pairs={{0,4},{4,8},{8,12},{12,16},{16,20},{20,24},{24,28},{28,32},{32,36}... | collective-permute-start | bytes 297992 | tf_op jit(solution)/shard_map/ppermute | solution.py:118
  23.4 0.6 copy-start.2
  24.0 0.7 slice-start.1
  26.8 0.7 slice-start
  27.5 0.7 copy-start.4
  29.8 15.1 %all-to-all-start = ((f32[64,1,544]{2,1,0:T(1,128)}), f32[64,1,544]{2,1,0:T(1,128)S(1)}, u32[]{:S(2)}, u32[]{:S(2)}) async-start(f32[64,1,544]{2,1,0:T(1,128)} %reshape.103), calls=%async_computation | async-start | bytes 327680 | tf_op jit(solution)/shard_map/all_to_all | solution.py:58
  34.8 84.4 %collective-permute-start.4 = (f32[32,3,16,128]{3,0,2,1:T(8,128)S(1)}, f32[32,3,16,128]{3,0,2,1:T(8,128)S(1)}, u32[]{:S(2)}, u32[]{:S(2)}) collective-permute-start(f32[32,3,16,128]{3,0,2,1:T(8,128)S(1)} %pad_maximum_fusion.1), channel_id=1, source_target_pairs={{0,3},{1,0},{2,1},{3,2},{4,7},{5,4},{6,5},{7,6},{8,11},{9,8},{10,9... | collective-permute-start | bytes 2359304 | tf_op jit(solution)/shard_map/ppermute | solution.py:171
  49.4 27.4 %all-to-all-start.1 = ((f32[16,17,128]{2,1,0:T(8,128)}), f32[16,17,128]{2,1,0:T(8,128)S(1)}, u32[]{:S(2)}, u32[]{:S(2)}) async-start(f32[16,17,128]{2,1,0:T(8,128)} %broadcast_in_dim.74), calls=%async_computation.1 | async-start | bytes 393216 | tf_op jit(solution)/shard_map/all_to_all | solution.py:58
  64.4 55.6 %collective-permute-start.2 = (f32[32,3,16,128]{3,0,2,1:T(8,128)S(1)}, f32[32,3,16,128]{3,0,2,1:T(8,128)}, u32[]{:S(2)}, u32[]{:S(2)}) collective-permute-start(f32[32,3,16,128]{3,0,2,1:T(8,128)S(1)} %pad_maximum_fusion.1), channel_id=1, source_target_pairs={{0,1},{1,2},{2,3},{3,0},{4,5},{5,6},{6,7},{7,4},{8,9},{9,10},{10,1... | collective-permute-start | bytes 2359304 | tf_op jit(solution)/shard_map/ppermute | solution.py:171
  66.6 55.4 %collective-permute-start.3 = (f32[32,3,16,128]{3,0,2,1:T(8,128)S(1)}, f32[32,3,16,128]{3,0,2,1:T(8,128)}, u32[]{:S(2)}, u32[]{:S(2)}) collective-permute-start(f32[32,3,16,128]{3,0,2,1:T(8,128)S(1)} %pad_maximum_fusion.1), channel_id=1, source_target_pairs={{0,2},{1,3},{2,0},{3,1},{4,6},{5,7},{6,4},{7,5},{8,10},{9,11},{10,... | collective-permute-start | bytes 2359304 | tf_op jit(solution)/shard_map/ppermute | solution.py:171
  77.5 27.1 %all-to-all-start.2 = ((f32[8,16,128]{2,1,0:T(8,128)}), f32[8,16,128]{2,1,0:T(8,128)S(1)}, u32[]{:S(2)}, u32[]{:S(2)}) async-start(f32[8,16,128]{2,1,0:T(8,128)} %broadcast_in_dim.75), calls=%async_computation.2 | async-start | bytes 131072 | tf_op jit(solution)/shard_map/all_to_all | solution.py:58
  104.6 0.6 copy-start.1
  117.6 1.6 %copy-start = (f32[128,128]{1,0:T(8,128)S(1)}, f32[128,128]{1,0:T(8,128)}, u32[]{:S(2)}) copy-start(f32[128,128]{1,0:T(8,128)} %shard_map.77) | copy-start | bytes 196612

commit v2 on v1

--- a/solution.py
+++ b/solution.py
@@ -60,63 +60,158 @@
     )
 
 
-def weights_kernel(gram_ref, project_ref, out_ref, left, right):
-    members = gram_ref.shape[0]
-    rows = lax.broadcasted_iota(jnp.int32, (members, members), 0)
-    cols = lax.broadcasted_iota(jnp.int32, (members, members), 1)
-    ident = jnp.where(rows == cols, 1.0, 0.0)
-    left[0:members, :] = gram_ref[...] + ident
-    right[0:members, :] = ident
-    left[members:, :] = jnp.broadcast_to(project_ref[...], (8, members))
-    right[members:, :] = jnp.zeros((8, members), jnp.float32)
-    total = members + 8
-    for j in range(members):
-        base = (j // 8) * 8
-        row_a = left[j : j + 1, :]
-        row_m = right[j : j + 1, :]
-        pivot = lax.rsqrt(row_a[:, j : j + 1])
-        scaled_a = row_a * pivot
-        scaled_m = row_m * pivot
-        column = left[base:total, j : j + 1] * pivot
-        position = lax.broadcasted_iota(jnp.int32, (total - base, 1), 0) + base
-        column = jnp.where(position > j, column, 0.0)
-        left[base:total, :] = left[base:total, :] - column * scaled_a
-        right[base:total, :] = right[base:total, :] - column * scaled_m
-        right[j : j + 1, :] = scaled_m
-    shift = -right[members : members + 1, :]
-    combined = right[0:members, :] + shift * (1.0 / (members - 1) ** 0.5)
-    mean = jnp.sum(combined, axis=1, keepdims=True) * (1.0 / members)
-    out_ref[...] = combined - mean + 1.0 / members
-
-
-def analysis_weights(gram, project):
-    members = gram.shape[0]
+def weights_kernel(mem_ref, gram_ref, project_ref, out_ref, work):
+    blocks, size, members = gram_ref.shape
+    shape = (size, members)
+    own = out_ref.shape[0]
+    lane = lax.broadcasted_iota(jnp.int32, shape, 1)
+    sub = lax.broadcasted_iota(jnp.int32, shape, 0)
+    slabs = [
+        gram_ref[k] + jnp.where(lane == sub + k * size, 1.0, 0.0) for k in range(blocks)
+    ]
+    slabs.append(jnp.broadcast_to(project_ref[...], shape))
+    for k in range(blocks):
+        base = k * size
+        inside = (lane >= base) & (lane < base + size)
+        slab = slabs[k]
+        columns = [
+            jnp.broadcast_to(slab[:, base + c : base + c + 1], shape) for c in range(size)
+        ]
+        entry = {
+            (c, r): jnp.broadcast_to(columns[c][r : r + 1], shape)
+            for c in range(size)
+            for r in range(c, size)
+        }
+        start = jnp.where(inside, jnp.where(lane == sub + base, 1.0, 0.0), slab)
+        rows = [jnp.broadcast_to(start[r : r + 1], shape) for r in range(size)]
+        scales = []
+        for j in range(size):
+            scale = lax.rsqrt(entry[j, j])
+            scales.append(scale)
+            rows[j] = rows[j] * scale
+            for i in range(j + 1, size):
+                entry[j, i] = entry[j, i] * scale
+            for i in range(j + 1, size):
+                rows[i] = rows[i] - entry[j, i] * rows[j]
+                for c in range(i, size):
+                    entry[i, c] = entry[i, c] - entry[j, i] * entry[j, c]
+        for i in range(k + 1, blocks + 1):
+            target = slabs[i]
+            kept = jnp.where(inside, 0.0, target)
+            factors = []
+            for j in range(size):
+                value = jnp.broadcast_to(target[:, base + j : base + j + 1], shape)
+                for c in range(j):
+                    value = value - factors[c] * entry[c, j]
+                value = value * scales[j]
+                factors.append(value)
+                kept = kept - value * rows[j]
+            slabs[i] = kept
+        final = rows[0]
+        for r in range(1, size):
+            final = jnp.where(sub == r, rows[r], final)
+        slabs[k] = jnp.where(lane < base + size, final, 0.0)
+    shift = slabs[blocks] * (-1.0 / (members - 1) ** 0.5)
+    for k in range(blocks):
+        combined = slabs[k] + shift
+        mean = jnp.sum(combined, axis=1, keepdims=True) * (1.0 / members)
+        work[k * size : (k + 1) * size, :] = combined - mean + 1.0 / members
+    first = pl.multiple_of(mem_ref[0] * own, own)
+    turn = lax.rem(members - first, members)
+    out_ref[...] = pltpu.roll(work[pl.ds(first, own), :], turn, 1)
+
+
+def analysis_weights(mem_index, gram, project, own):
+    members = gram.shape[2]
     return pl.pallas_call(
         weights_kernel,
-        out_shape=jax.ShapeDtypeStruct((members, members), jnp.float32),
-        scratch_shapes=[
-            pltpu.VMEM((members + 8, members), jnp.float32),
-            pltpu.VMEM((members + 8, members), jnp.float32),
+        out_shape=jax.ShapeDtypeStruct((own, members), jnp.float32),
+        in_specs=[
+            pl.BlockSpec(memory_space=pltpu.SMEM),
+            pl.BlockSpec(memory_space=pltpu.VMEM),
+            pl.BlockSpec(memory_space=pltpu.VMEM),
         ],
-    )(gram, project)
+        out_specs=pl.BlockSpec(memory_space=pltpu.VMEM),
+        scratch_shapes=[pltpu.VMEM((members, members), jnp.float32)],
+    )(mem_index.reshape(1), gram, project)
+
+
+def mix_kernel(weights_ref, *refs):
+    *sources, pair_ref, speed_ref = refs
+    kinds, depth, members, width = sources[0].shape
+    weights = weights_ref[...]
+    high = weights.astype(jnp.bfloat16)
+    low = (weights - high.astype(jnp.float32)).astype(jnp.bfloat16)
+    both = jnp.concatenate([high, low], axis=0)
+    for kind in range(kinds):
+        for row in range(0, depth, 2):
+            tile = jnp.concatenate(
+                [
+                    jnp.concatenate(
+                        [source[kind, row + i] for source in sources], axis=0
+                    )
+                    for i in range(2)
+                ],
+                axis=1,
+            )
+            tile_high = tile.astype(jnp.bfloat16)
+            tile_low = (tile - tile_high.astype(jnp.float32)).astype(jnp.bfloat16)
+            main = jnp.dot(both, tile_high, preferred_element_type=jnp.float32)
+            rest = jnp.dot(high, tile_low, preferred_element_type=jnp.float32)
+            result = main[:members] + (main[members:] + rest)
+            for i in range(2):
+                part = result[:, i * width : (i + 1) * width]
+                if kind < 2:
+                    pair_ref[:, kind, row + i, :] = part
+                else:
+                    speed_ref[:, row + i, :] = part
+
+
+def mix(weights, sources):
+    groups = len(sources)
+    kinds, depth, members, width = sources[0].shape
+    return pl.pallas_call(
+        mix_kernel,
+        grid=(2,),
+        in_specs=[
+            pl.BlockSpec((members, groups * members), lambda i: (0, 0)),
+        ]
+        + [pl.BlockSpec((kinds, depth // 2, members, width), lambda i: (0, i, 0, 0))] * groups,
+        out_specs=[
+            pl.BlockSpec((members, 2, depth // 2, width), lambda i: (0, 0, i, 0)),
+            pl.BlockSpec((members, depth // 2, width), lambda i: (0, i, 0)),
+        ],
+        out_shape=[
+            jax.ShapeDtypeStruct((members, 2, depth, width), jnp.float32),
+            jax.ShapeDtypeStruct((members, depth, width), jnp.float32),
+        ],
+        compiler_params=pltpu.CompilerParams(vmem_limit_bytes=24 * 1024 * 1024),
+    )(weights, *sources)
 
 
 def on_device(member_heat_solute, velocity, phase_mask, obs_index, obs_value, obs_error):
     members, _, depth, width = member_heat_solute.shape
     mushy = phase_mask.astype(jnp.float32)
-    fields = jnp.concatenate(
-        [
-            member_heat_solute[:, 0],
-            member_heat_solute[:, 1],
-            velocity,
-            mushy[None],
-        ],
-        axis=0,
-    )
     count = lax.axis_size(SPACE)
     position = lax.axis_index(SPACE)
-    above = lax.ppermute(fields[:, -2:], SPACE, [(i, i + 1) for i in range(count - 1)])
-    below = lax.ppermute(fields[:, :2], SPACE, [(i + 1, i) for i in range(count - 1)])
+
+    def edge(first):
+        rows = slice(first, first + 2)
+        return jnp.concatenate(
+            [
+                member_heat_solute[:, 0, rows],
+                member_heat_solute[:, 1, rows],
+                velocity[:, rows],
+                mushy[None, rows],
+            ],
+            axis=0,
+        )
+
+    above = lax.ppermute(edge(depth - 2), SPACE, [(i, i + 1) for i in range(count - 1)])
+    below = lax.ppermute(edge(0), SPACE, [(i + 1, i) for i in range(count - 1)])
+    fields = jnp.concatenate(
+        [member_heat_solute[:, 0], member_heat_solute[:, 1], velocity, mushy[None]], axis=0
+    )
     padded = jnp.concatenate([above, fields, below], axis=1)
     mushy = padded[3 * members]
     factor = 1.0 - mushy * (1.0 - mushy_ratio)
@@ -151,33 +246,23 @@
         error[:, None] * jnp.sqrt(jnp.float32(ensemble - 1))
     )
     innovation = (value - mean_obs) / error
-    pieces = mem_size * lax.axis_size("core")
-    piece = lax.axis_index("mem") * lax.axis_size("core") + lax.axis_index("core")
+    pieces = lax.axis_size(("y", "core"))
+    piece = lax.axis_index(("y", "core"))
     height = ensemble // pieces
     own_cols = lax.dynamic_slice_in_dim(spread, piece * height, height, 1)
     left = jnp.concatenate([own_cols, innovation[:, None]], axis=1)
     part = lax.dot_general(left, spread, (((0,), (0,)), ((), ())), precision=HIGHEST)
     part = jnp.sum(shared(part, "z"), axis=0)
     project = part[height:]
-    gram = shared(part[:height], ("mem", "core")).reshape(ensemble, ensemble)
-    weights = analysis_weights(gram, project)
-
+    gram = shared(part[:height], ("y", "core"))
     mem_index = lax.axis_index("mem")
-    weights = lax.dynamic_slice_in_dim(weights, mem_index * members, members, 0)
-    states = jnp.stack([heat, solute, speed], axis=1)
-    result = None
-    for step in range(mem_size):
-        if step:
-            source = lax.ppermute(
-                states, "mem", [(i, (i + step) % mem_size) for i in range(mem_size)]
-            )
-        else:
-            source = states
-        origin = (mem_index - step + mem_size) % mem_size
-        block = lax.dynamic_slice_in_dim(weights, origin * members, members, 1)
-        term = jnp.einsum("kfzw,jk->jfzw", source, block, precision=HIGHEST)
-        result = term if result is None else result + term
-    return (result[:, :2], result[:, 2])
+    weights = analysis_weights(mem_index, gram, project, members)
+    states = jnp.stack([heat, solute, speed], axis=0).transpose(0, 2, 1, 3)
+    sources = [states]
+    for step in range(1, mem_size):
+        pairs = [((i + step) % mem_size, i) for i in range(mem_size)]
+        sources.append(lax.ppermute(states, "mem", pairs))
+    return mix(weights, sources)
 
 
 def solution(mesh):

time: 127 us -> 111 us (0.87)
  blocking collectives: 0 us -> 26.8 us
  waiting for transfers between devices: 30.7 us -> 8.53 us
  starting transfers between devices: 57.3 us -> 42.6 us
  matrix products: 6.9 us -> 0.53 us
  Pallas kernels: 12.4 us -> 7.49 us
  local copies, waits for them, and re-layouts: 13.1 us -> 17 us
  other arithmetic: 4.47 us -> 6.12 us
    all_to_all x0 -> x1, blocking collectives: none -> 26.8 us  [shared(): lax.all_to_all(jnp.broadcast_to(value[None], (count,) + value.shape), axe...]
    all_to_all x3 -> x2, waiting for transfers between devices: 29.3 us -> 7.28 us  [shared(): lax.all_to_all(jnp.broadcast_to(value[None], (count,) + value.shape), axe...]
    all_to_all x3 -> x2, starting transfers between devices: 28.6 us -> 15.2 us  [shared(): lax.all_to_all(jnp.broadcast_to(value[None], (count,) + value.shape), axe...]
    dot_general x4 -> x0, matrix products: 6.38 us -> none  [on_device(): term = jnp.einsum('kfzw,jk->jfzw', source, block, precision=HIGHEST)]
    pallas_call x1 -> x2, Pallas kernels: 12.4 us -> 7.49 us  [the longest x1 5.55 us: analysis_weights(): pl.pallas_call(weights_kernel, out_shape=jax.ShapeDtypeStruct((own, membe...]
    transpose x2, local copies, waits for them, and re-layouts: 0.24 us -> 4.01 us  [on_device(): arrived[..., :members].transpose(0, 2, 1, 3)]
    ppermute x5, starting transfers between devices: 28.8 us -> 27.5 us  [the longest x1 16.1 us: on_device(): below = lax.ppermute(edge(0), SPACE, [(i + 1, i) for i in range(count - 1)])]
    unnamed x23 -> x27, local copies, waits for them, and re-layouts: 5.78 us -> 5.23 us
  transfers between devices with their start and end apart: 8 -> 7, of which waited for: 4 -> 2; matrix products, arithmetic and copies ran while one was open for 8% -> 11% of each run, Pallas kernels for 10% -> 5%
where the time goes in v2:
time: 111 us; the launch traced here: 110 us
  starting transfers between devices  42.6 us (38%)
  blocking collectives  26.8 us (24%)
  local copies, waits for them, and re-layouts  17 us (15%)
  waiting for transfers between devices  8.53 us (8%)
  Pallas kernels  7.49 us (7%)
  other arithmetic  6.12 us (6%)
    all_to_all x1, blocking collectives, shared(): lax.all_to_all(jnp.broadcast_to(value[None], (count,) + value.shape), axe...  26.8 us
    ppermute x1, starting transfers between devices, on_device(): below = lax.ppermute(edge(0), SPACE, [(i + 1, i) for i in range(count - 1)])  16.1 us
    all_to_all x2, starting transfers between devices, shared(): lax.all_to_all(jnp.broadcast_to(value[None], (count,) + value.shape), axe...  15.2 us
    ppermute x3, starting transfers between devices, on_device(): sources.append(lax.ppermute(states, 'mem', pairs))  9.47 us
    all_to_all x2, waiting for transfers between devices, shared(): lax.all_to_all(jnp.broadcast_to(value[None], (count,) + value.shape), axe...  7.28 us
    pallas_call x1, Pallas kernels, analysis_weights(): pl.pallas_call(weights_kernel, out_shape=jax.ShapeDtypeStruct((own, membe...  5.55 us
    unnamed x27, local copies, waits for them, and re-layouts  5.23 us
    transpose x2, local copies, waits for them, and re-layouts, on_device(): arrived[..., :members].transpose(0, 2, 1, 3)  4.01 us
  transfers between devices with their start and end apart: 7, of which 2 were waited for; matrix products, arithmetic and copies ran while one was open for 11% of the time, Pallas kernels for 5%

profile of v2, /device:TPU:1, one launch (start us, length us, event | category | flops | bytes accessed | tf_op | source)
XLA Modules:
  0.0 110.2 jit_solution(4662230810624504783)
XLA Ops:
  0.6 0.8 convert_element_type.3
  1.4 1.0 copy.91
  2.5 1.2 %fusion.67 = (f32[32,1,2,128]{3,2,1,0:T(2,128)S(1)}, f32[32,1,2,128]{3,2,1,0:T(2,128)S(1)}, f32[32,1,2,128]{3,2,1,0:T(2,128)S(1)}, f32[32,1,2,128]{3,2,1,0:T(2,128)S(1)}) fusion(f32[32,2,16,128]{3,2,1,0:T(8,128)} %param.6), kind=kLoop, calls=%fused_computation.122 | loop fusion | bytes 262144 | tf_op jit(solution)/shard_map/slice | solution.py:202
  3.7 16.1 %collective-permute-start.1 = (f32[97,2,128]{2,0,1:T(8,128)S(1)}, f32[97,2,128]{2,0,1:T(8,128)S(1)}, u32[]{:S(2)}, u32[]{:S(2)}) collective-permute-start(f32[97,2,128]{2,0,1:T(8,128)S(1)} %pad_maximum_fusion.10), channel_id=1, source_target_pairs={{4,0},{8,4},{12,8},{16,12},{20,16},{24,20},{28,24},{32,28},{36,32}... | collective-permute-start | bytes 297992 | tf_op jit(solution)/shard_map/ppermute | solution.py:211
  19.8 1.9 %collective-permute-start = (f32[97,2,128]{2,0,1:T(8,128)S(1)}, f32[97,2,128]{2,0,1:T(8,128)S(1)}, u32[]{:S(2)}, u32[]{:S(2)}) collective-permute-start(f32[97,2,128]{2,0,1:T(8,128)S(1)} %pad_maximum_fusion.9), channel_id=1, source_target_pairs={{0,4},{4,8},{8,12},{12,16},{16,20},{20,24},{24,28},{28,32},{32,36}... | collective-permute-start | bytes 297992 | tf_op jit(solution)/shard_map/ppermute | solution.py:210
  22.2 1.2 %collective-permute-done = f32[97,2,128]{2,0,1:T(8,128)S(1)} collective-permute-done((f32[97,2,128]{2,0,1:T(8,128)S(1)}, f32[97,2,128]{2,0,1:T(8,128)S(1)}, u32[]{:S(2)}, u32[]{:S(2)}) %collective-permute-start) | collective-permute-done | bytes 99360 | tf_op jit(solution)/shard_map/ppermute | solution.py:210
  23.5 0.5 copy-done.5
  24.8 0.5 slice-done.1
  25.9 0.3 fusion.7
  27.0 0.8 fusion.72
  27.8 1.0 multiply_bitcast_fusion
  29.3 1.1 %reshape.99 = f32[64,1,544]{2,1,0:T(1,128)} reshape(f32[64,16,34]{2,1,0:T(8,128)S(1)} %broadcast_in_dim.81) | data formatting | bytes 278528
  30.5 4.6 %all-to-all-start = ((f32[64,1,544]{2,1,0:T(1,128)}), f32[64,1,544]{2,1,0:T(1,128)S(1)}, u32[]{:S(2)}, u32[]{:S(2)}) async-start(f32[64,1,544]{2,1,0:T(1,128)} %reshape.99), calls=%async_computation | async-start | bytes 327680 | tf_op jit(solution)/shard_map/all_to_all | solution.py:58
  35.1 1.5 %fusion.39 = (f32[1,32,16,128]{3,1,2,0:T(8,128)S(1)}, f32[1,32,16,128]{3,1,2,0:T(8,128)S(1)}) fusion(f32[32,18,128]{2,0,1:T(8,128)S(1)} %fusion.7, f32[32,16,127]{2,0,1:T(8,128)S(1)} %get-tuple-element.32, f32[32,16,1]{2,0,1:T(8,128)S(1)} %get-tuple-element.34, f32[32,16,1]{2,0,1:T(8,128)S(1)} %get-tuple-element.33, ...), kind=kLoop, calls=%fused_computation.60 | loop fusion | flops 1900544 | bytes 3424256 | tf_op jit(solution)/shard_map/stack | solution.py:260
  36.7 4.5 %collective-permute-start.2 = (f32[3,16,32,128]{3,2,1,0:T(8,128)S(1)}, f32[3,16,32,128]{3,2,1,0:T(8,128)S(1)}, u32[]{:S(2)}, u32[]{:S(2)}) collective-permute-start(f32[3,16,32,128]{3,2,1,0:T(8,128)S(1)} %maximum_bitcast_fusion.refs_0_), channel_id=1, source_target_pairs={{1,0},{2,1},{3,2},{0,3},{5,4},{6,5},{7,6},{4,7},{9,8},{10,9},{11,1... | collective-permute-start | bytes 2359304 | tf_op jit(solution)/shard_map/ppermute | solution.py:264
  41.2 2.5 %collective-permute-start.3 = (f32[3,16,32,128]{3,2,1,0:T(8,128)S(1)}, f32[3,16,32,128]{3,2,1,0:T(8,128)S(1)}, u32[]{:S(2)}, u32[]{:S(2)}) collective-permute-start(f32[3,16,32,128]{3,2,1,0:T(8,128)S(1)} %maximum_bitcast_fusion.refs_0_), channel_id=1, source_target_pairs={{2,0},{3,1},{0,2},{1,3},{6,4},{7,5},{4,6},{5,7},{10,8},{11,9},{8,1... | collective-permute-start | bytes 2359304 | tf_op jit(solution)/shard_map/ppermute | solution.py:264
  43.7 2.5 %collective-permute-start.4 = (f32[3,16,32,128]{3,2,1,0:T(8,128)S(1)}, f32[3,16,32,128]{3,2,1,0:T(8,128)S(1)}, u32[]{:S(2)}, u32[]{:S(2)}) collective-permute-start(f32[3,16,32,128]{3,2,1,0:T(8,128)S(1)} %maximum_bitcast_fusion.refs_0_), channel_id=1, source_target_pairs={{3,0},{0,1},{1,2},{2,3},{7,4},{4,5},{5,6},{6,7},{11,8},{8,9},{9,10... | collective-permute-start | bytes 2359304 | tf_op jit(solution)/shard_map/ppermute | solution.py:264
  46.2 0.5 broadcast.86
  46.7 1.0 reduce.7
  47.7 1.2 %reshape.100 = f32[64,16,34]{2,1,0:T(8,128)} reshape(f32[64,544]{1,0:T(8,128)S(1)} %reduce.7) | data formatting | bytes 278528
  48.9 2.0 %slice_bitcast_fusion = f32[16,16,4,32]{3,1,2,0:T(8,128)} fusion(f32[16,4,16,34]{3,2,1,0:T(8,128)} %bitcast.53), kind=kLoop, calls=%fused_computation.2 | loop fusion | bytes 262144 | tf_op jit(solution)/shard_map/transpose | solution.py:241
  51.4 2.0 %copy.103 = f32[16,16,4,32]{3,2,1,0:T(4,128)} copy(f32[16,16,4,32]{3,1,2,0:T(8,128)} %slice_bitcast_fusion) | data formatting | bytes 262144 | tf_op jit(solution)/shard_map/transpose | solution.py:241
  53.5 1.3 %reshape.95 = f32[256,128]{1,0:T(8,128)S(1)} reshape(f32[16,16,4,32]{3,2,1,0:T(4,128)} %copy.103) | data formatting | bytes 262144 | tf_op jit(solution)/shard_map/reshape | solution.py:241
  55.6 26.8 %all_to_all.15 = f32[16,9,128]{2,1,0:T(8,128)S(1)} all-to-all(f32[16,9,128]{2,1,0:T(8,128)S(1)} %broadcast_in_dim.82), channel_id=1, replica_groups=mesh['z'=16,'y'=8,'core'=2,'mem'=4] {'z'}, dimensions={0} | all-to-all | bytes 147456 | tf_op jit(solution)/shard_map/all_to_all | solution.py:58
  82.4 0.6 broadcast_in_dim.83
  83.0 10.5 %all-to-all-start.2 = ((f32[16,8,128]{2,1,0:T(8,128)}), f32[16,8,128]{2,1,0:T(8,128)S(1)}, u32[]{:S(2)}, u32[]{:S(2)}) async-start(f32[16,8,128]{2,1,0:T(8,128)} %broadcast_in_dim.83), calls=%async_computation.2 | async-start | bytes 131072 | tf_op jit(solution)/shard_map/all_to_all | solution.py:58
  93.6 0.5 slice.360.project_ref
  94.1 7.3 %all-to-all-done.2.gram_ref = f32[16,8,128]{2,1,0:T(8,128)S(1)} async-done(((f32[16,8,128]{2,1,0:T(8,128)}), f32[16,8,128]{2,1,0:T(8,128)S(1)}, u32[]{:S(2)}, u32[]{:S(2)}) %all-to-all-start.2) | async-done | bytes 65568 | tf_op jit(solution)/shard_map/all_to_all | solution.py:58
  101.4 0.6 copy-done.4
  102.0 5.5 %shard_map.77.weights_ref = f32[32,128]{1,0:T(8,128)} custom-call(s32[1]{0:T(128)} %bitcast.mem_ref, f32[16,8,128]{2,1,0:T(8,128)} %copy-done.4, f32[1,128]{1,0:T(1,128)} %slice.360.project_ref), custom_call_target="tpu_custom_call" | custom-call | tf_op jit(solution)/shard_map/pallas_call | solution.py:126
  107.6 0.7 copy-done
  108.3 1.9 %shard_map.78 = (f32[32,2,16,128]{3,2,1,0:T(8,128)}, f32[32,16,128]{2,1,0:T(8,128)}) custom-call(f32[32,128]{1,0:T(8,128)S(1)} %copy-done, f32[3,16,32,128]{3,2,1,0:T(8,128)S(1)} %maximum_bitcast_fusion.refs_0_, f32[3,16,32,128]{3,2,1,0:T(8,128)S(1)} %collective-permute-done.2.refs_1_, f32[3,16,32,128]{3,2,1,0:T(8,128)S(1)} %collective-permute-done.3.refs_2_, ...), custom_call_target="tpu_custom_call" | custom-call | tf_op jit(solution)/shard_map/pallas_call | solution.py:173
  (77 shorter events, 4.6 us)
Async XLA Ops:
  0.6 21.1 %copy-start.3 = (f32[32,2,16,128]{3,2,1,0:T(8,128)S(1)}, f32[32,2,16,128]{3,2,1,0:T(8,128)}, u32[]{:S(2)}) copy-start(f32[32,2,16,128]{3,2,1,0:T(8,128)} %param.6) | copy-start | bytes 1572868
  2.4 19.3 %copy-start.6 = (s32[16,128]{1,0:T(8,128)S(1)}, s32[16,128]{1,0:T(8,128)}, u32[]{:S(2)}) copy-start(s32[16,128]{1,0:T(8,128)} %param.8) | copy-start | bytes 24580
  2.5 19.3 %copy-start.8 = (f32[16]{0:T(128)S(1)}, f32[16]{0:T(128)}, u32[]{:S(2)}) copy-start(f32[16]{0:T(128)} %param.11) | copy-start | bytes 196
  2.5 19.4 %copy-start.9 = (f32[16]{0:T(128)S(1)}, f32[16]{0:T(128)}, u32[]{:S(2)}) copy-start(f32[16]{0:T(128)} %param.10) | copy-start | bytes 196
  3.7 18.5 %collective-permute-start.1 = (f32[97,2,128]{2,0,1:T(8,128)S(1)}, f32[97,2,128]{2,0,1:T(8,128)S(1)}, u32[]{:S(2)}, u32[]{:S(2)}) collective-permute-start(f32[97,2,128]{2,0,1:T(8,128)S(1)} %pad_maximum_fusion.10), channel_id=1, source_target_pairs={{4,0},{8,4},{12,8},{16,12},{20,16},{24,20},{28,24},{32,28},{36,32}... | collective-permute-start | bytes 297992 | tf_op jit(solution)/shard_map/ppermute | solution.py:211
  19.8 3.6 %collective-permute-start = (f32[97,2,128]{2,0,1:T(8,128)S(1)}, f32[97,2,128]{2,0,1:T(8,128)S(1)}, u32[]{:S(2)}, u32[]{:S(2)}) collective-permute-start(f32[97,2,128]{2,0,1:T(8,128)S(1)} %pad_maximum_fusion.9), channel_id=1, source_target_pairs={{0,4},{4,8},{8,12},{12,16},{16,20},{20,24},{24,28},{28,32},{32,36}... | collective-permute-start | bytes 297992 | tf_op jit(solution)/shard_map/ppermute | solution.py:210
  23.4 0.6 copy-start.5
  24.6 0.7 slice-start.1
  26.9 0.9 slice-start
  27.8 1.0 copy-start.7
  30.5 15.7 %all-to-all-start = ((f32[64,1,544]{2,1,0:T(1,128)}), f32[64,1,544]{2,1,0:T(1,128)S(1)}, u32[]{:S(2)}, u32[]{:S(2)}) async-start(f32[64,1,544]{2,1,0:T(1,128)} %reshape.99), calls=%async_computation | async-start | bytes 327680 | tf_op jit(solution)/shard_map/all_to_all | solution.py:58
  35.1 1.5 %copy-start.2 = (f32[32,16,128]{2,0,1:T(8,128)S(1)}, f32[32,16,128]{2,0,1:T(8,128)}, u32[]{:S(2)}) copy-start(f32[32,16,128]{2,0,1:T(8,128)} %get-tuple-element.8) | copy-start | bytes 786436
  36.7 70.9 %collective-permute-start.2 = (f32[3,16,32,128]{3,2,1,0:T(8,128)S(1)}, f32[3,16,32,128]{3,2,1,0:T(8,128)S(1)}, u32[]{:S(2)}, u32[]{:S(2)}) collective-permute-start(f32[3,16,32,128]{3,2,1,0:T(8,128)S(1)} %maximum_bitcast_fusion.refs_0_), channel_id=1, source_target_pairs={{1,0},{2,1},{3,2},{0,3},{5,4},{6,5},{7,6},{4,7},{9,8},{10,9},{11,1... | collective-permute-start | bytes 2359304 | tf_op jit(solution)/shard_map/ppermute | solution.py:264
  41.2 66.4 %collective-permute-start.3 = (f32[3,16,32,128]{3,2,1,0:T(8,128)S(1)}, f32[3,16,32,128]{3,2,1,0:T(8,128)S(1)}, u32[]{:S(2)}, u32[]{:S(2)}) collective-permute-start(f32[3,16,32,128]{3,2,1,0:T(8,128)S(1)} %maximum_bitcast_fusion.refs_0_), channel_id=1, source_target_pairs={{2,0},{3,1},{0,2},{1,3},{6,4},{7,5},{4,6},{5,7},{10,8},{11,9},{8,1... | collective-permute-start | bytes 2359304 | tf_op jit(solution)/shard_map/ppermute | solution.py:264
  43.7 63.9 %collective-permute-start.4 = (f32[3,16,32,128]{3,2,1,0:T(8,128)S(1)}, f32[3,16,32,128]{3,2,1,0:T(8,128)S(1)}, u32[]{:S(2)}, u32[]{:S(2)}) collective-permute-start(f32[3,16,32,128]{3,2,1,0:T(8,128)S(1)} %maximum_bitcast_fusion.refs_0_), channel_id=1, source_target_pairs={{3,0},{0,1},{1,2},{2,3},{7,4},{4,5},{5,6},{6,7},{11,8},{8,9},{9,10... | collective-permute-start | bytes 2359304 | tf_op jit(solution)/shard_map/ppermute | solution.py:264
  48.9 2.0 %copy-start.1 = (f32[64,16,34]{2,1,0:T(8,128)S(1)}, f32[64,16,34]{2,1,0:T(8,128)}, u32[]{:S(2)}) copy-start(f32[64,16,34]{2,1,0:T(8,128)} %reshape.100) | copy-start | bytes 417796
  83.0 18.3 %all-to-all-start.2 = ((f32[16,8,128]{2,1,0:T(8,128)}), f32[16,8,128]{2,1,0:T(8,128)S(1)}, u32[]{:S(2)}, u32[]{:S(2)}) async-start(f32[16,8,128]{2,1,0:T(8,128)} %broadcast_in_dim.83), calls=%async_computation.2 | async-start | bytes 131072 | tf_op jit(solution)/shard_map/all_to_all | solution.py:58
  101.4 0.6 copy-start.4
  107.6 0.7 copy-start

commit v3 on v2

--- a/solution.py
+++ b/solution.py
@@ -18,46 +18,249 @@
 HIGHEST = lax.Precision.HIGHEST
 
 
-def lateral(field):
-    left = jnp.concatenate([field[..., :1], field[..., :-1]], axis=-1)
-    right = jnp.concatenate([field[..., 1:], field[..., -1:]], axis=-1)
+def lateral(field, lane):
+    last = field.shape[1] - 1
+    left = jnp.where(lane == 0, field, pltpu.roll(field, 1, 1))
+    right = jnp.where(lane == last, field, pltpu.roll(field, last, 1))
     return left + right - 2.0 * field
 
 
-def laplacian(padded):
-    centre = padded[:, 1:-1]
-    return padded[:, 2:] + padded[:, :-2] - 2.0 * centre + lateral(centre)
-
-
-def advance(heat, solute, speed, mushy, factor):
-    temp = heat * factor
-    inner_heat = heat[:, 1:-1]
-    inner_solute = solute[:, 1:-1]
-    inner_speed = speed[:, 1:-1]
-    inner_mushy = mushy[1:-1]
-    carried = advection * inner_speed
-    new_heat = (
-        inner_heat + heat_diffusion * laplacian(temp) - carried * (inner_heat - heat[:, :-2])
+def advance(heat, temp, solute, speed, mushy, lane):
+    def laplacian(rows):
+        return rows[2] + rows[0] - 2.0 * rows[1] + lateral(rows[1], lane)
+
+    carried = advection * speed[1]
+    new_heat = heat[1] + heat_diffusion * laplacian(temp) - carried * (heat[1] - heat[0])
+    new_solute = (
+        solute[1]
+        + solute_diffusion * laplacian(solute)
+        - carried * (solute[1] - solute[0])
+        + segregation * mushy * (temp[1] - solute[1])
     )
-    new_solute = (
-        inner_solute
-        + solute_diffusion * laplacian(solute)
-        - carried * (inner_solute - solute[:, :-2])
-        + segregation * inner_mushy * (temp[:, 1:-1] - inner_solute)
+    new_speed = speed[1] + momentum_diffusion * laplacian(speed) - darcy_drag * mushy * speed[1]
+    return new_heat, new_solute, new_speed
+
+
+def edge_kernel(pair_ref, speed_ref, mask_ref, tail_ref, head_ref):
+    depth = mask_ref.shape[0]
+    members = speed_ref.shape[0] // depth
+    for out_ref, first in ((tail_ref, depth - 2), (head_ref, 0)):
+        for i in range(2):
+            row = first + i
+            for kind in range(3):
+                if kind < 2:
+                    part = pair_ref[pl.ds(kind * depth + row, members, stride=2 * depth), :]
+                else:
+                    part = speed_ref[pl.ds(row, members, stride=depth), :]
+                place = (i * 3 + kind) * members
+                out_ref[place : place + members, :] = part
+        place = 6 * members
+        out_ref[place : place + 8, :] = jnp.zeros((8, out_ref.shape[1]), jnp.float32)
+        out_ref[place : place + 2, :] = mask_ref[first : first + 2, :].astype(jnp.float32)
+
+
+def edges(pair, speed, mask):
+    members = speed.shape[0] // mask.shape[0]
+    shape = jax.ShapeDtypeStruct((6 * members + 8, mask.shape[1]), jnp.float32)
+    return pl.pallas_call(edge_kernel, out_shape=[shape, shape])(pair, speed, mask)
+
+
+def forecast_kernel(
+    ends_ref, index_ref, value_ref, error_ref, pair_ref, speed_ref, mask_ref, above_ref,
+    below_ref, states_ref, message_ref, middle, temps
+):
+    depth, width = mask_ref.shape
+    members = states_ref.shape[2]
+    n_obs = index_ref.shape[0]
+    lane = lax.broadcasted_iota(jnp.int32, (members, width), 1)
+
+    def outer(kind, row):
+        if row < 0:
+            place = ((row + 2) * 3 + kind) * members
+            return above_ref[place : place + members, :]
+        if row >= depth:
+            place = ((row - depth) * 3 + kind) * members
+            return below_ref[place : place + members, :]
+        if kind < 2:
+            return pair_ref[pl.ds(kind * depth + row, members, stride=2 * depth), :]
+        return speed_ref[pl.ds(row, members, stride=depth), :]
+
+    def mushy_at(row):
+        place = 6 * members
+        if row < 0:
+            return above_ref[place + row + 2 : place + row + 3, :]
+        if row >= depth:
+            return below_ref[place + row - depth : place + row - depth + 1, :]
+        return mask_ref[row : row + 1, :].astype(jnp.float32)
+
+    def inner(kind, row):
+        return middle[kind, row + 1]
+
+    mushy = {row: mushy_at(row) for row in range(-2, depth + 2)}
+    factor = {row: 1.0 - m * (1.0 - mushy_ratio) for row, m in mushy.items()}
+
+    def sweep(get, first, last, put):
+        heat = {r: get(0, r) for r in (first - 1, first)}
+        solute = {r: get(1, r) for r in (first - 1, first)}
+        speed = {r: get(2, r) for r in (first - 1, first)}
+        temp = {r: heat[r] * factor[r] for r in heat}
+        for row in range(first, last):
+            heat[row + 1] = get(0, row + 1)
+            solute[row + 1] = get(1, row + 1)
+            speed[row + 1] = get(2, row + 1)
+            temp[row + 1] = heat[row + 1] * factor[row + 1]
+            near = range(row - 1, row + 2)
+            put(
+                row,
+                advance(
+                    [heat[r] for r in near],
+                    [temp[r] for r in near],
+                    [solute[r] for r in near],
+                    [speed[r] for r in near],
+                    mushy[row],
+                    lane,
+                ),
+            )
+
+    def keep(row, new):
+        for kind in range(3):
+            part = new[kind]
+            if row < 0:
+                part = jnp.where(ends_ref[0] == 1, 0.0, part)
+            if row >= depth:
+                part = jnp.where(ends_ref[1] == 1, 0.0, part)
+            middle[kind, row + 1] = part
+
+    def finish(row, new):
+        for kind in range(3):
+            states_ref[kind, row] = new[kind]
+        temps[row] = new[0] * factor[row]
+
+    sweep(outer, -1, depth + 1, keep)
+    sweep(inner, 0, depth, finish)
+
+    root = float(4 * members - 1) ** 0.5
+    seen = jnp.zeros((members, width), jnp.float32)
+    for o in range(n_obs):
+        cell = index_ref[o]
+        tile = temps[cell // width]
+        column = jnp.sum(jnp.where(lane == cell % width, tile, 0.0), axis=1, keepdims=True)
+        scale = jnp.full((members, 1), error_ref[o], jnp.float32) * root
+        place = (o // 4) * 8 + o % 4
+        seen = jnp.where(lane == place, (column - value_ref[o]) / scale, seen)
+    square = jnp.concatenate(
+        [seen, jnp.zeros((width - members, width), jnp.float32)], axis=0
+    ).T
+    packed = square[0:8]
+    for q in range(1, n_obs // 4):
+        packed = packed + pltpu.roll(square[q * 8 : q * 8 + 8], q * members, 1)
+    for peer in range(message_ref.shape[0]):
+        message_ref[peer] = packed[0:4]
+
+
+def forecast(ends, obs_index, obs_value, obs_error, pair, speed, mask, above, below, peers):
+    depth, width = mask.shape
+    members = speed.shape[0] // depth
+    scalar = pl.BlockSpec(memory_space=pltpu.SMEM)
+    whole = pl.BlockSpec(memory_space=pltpu.VMEM)
+    return pl.pallas_call(
+        forecast_kernel,
+        in_specs=[scalar] * 4 + [whole] * 5,
+        out_specs=[whole, whole],
+        out_shape=[
+            jax.ShapeDtypeStruct((3, depth, members, width), jnp.float32),
+            jax.ShapeDtypeStruct((peers, 4, width), jnp.float32),
+        ],
+        scratch_shapes=[
+            pltpu.VMEM((3, depth + 2, members, width), jnp.float32),
+            pltpu.VMEM((depth, members, width), jnp.float32),
+        ],
+        compiler_params=pltpu.CompilerParams(vmem_limit_bytes=24 * 1024 * 1024),
+    )(ends, obs_index, obs_value, obs_error, pair, speed, mask, above, below)
+
+
+def gram_kernel(piece_ref, arrived_ref, states_ref, out_ref, passed_ref, work):
+    del states_ref, passed_ref
+    total, width = arrived_ref.shape
+    slabs = total // 16
+    share = width // 4
+    lane = lax.broadcasted_iota(jnp.int32, (slabs, width), 1)
+    blocks = []
+    for a in range(4):
+        held = [arrived_ref[pl.ds(m * 4 + a, slabs, stride=16), :] for m in range(4)]
+        for q in range(4):
+            block = pltpu.roll(held[0], (-q * share) % width, 1) if q else held[0]
+            for m in range(1, 4):
+                turn = ((m - q) * share) % width
+                part = pltpu.roll(held[m], turn, 1) if turn else held[m]
+                block = jnp.where(lane // share == m, part, block)
+            blocks.append(block)
+    scaled = jnp.concatenate(blocks, axis=0)
+    mean = jnp.sum(scaled, axis=1, keepdims=True) * (1.0 / width)
+    spread = scaled - mean
+    innovation = mean * -(float(width - 1) ** 0.5)
+    work[...] = lax.dot_general(
+        spread, spread, (((0,), (0,)), ((), ())), precision=HIGHEST,
+        preferred_element_type=jnp.float32,
     )
-    new_speed = (
-        inner_speed
-        + momentum_diffusion * laplacian(speed)
-        - darcy_drag * inner_mushy * inner_speed
-    )
-    return new_heat, new_solute, new_speed
-
-
-def shared(value, axes):
-    count = lax.axis_size(axes)
-    return lax.all_to_all(
-        jnp.broadcast_to(value[None], (count,) + value.shape), axes, 0, 0
-    )
+    project = jnp.sum(spread * innovation, axis=0, keepdims=True)
+    height = out_ref.shape[1] - 1
+    first = piece_ref[0] * height
+    for r in range(height):
+        row = work[pl.ds(first + r, 1), :]
+        for i in range(out_ref.shape[0]):
+            out_ref[i, r] = row
+    for i in range(out_ref.shape[0]):
+        out_ref[i, height] = project
+
+
+def gram_part(piece, arrived, states, peers, height):
+    width = arrived.shape[1]
+    return pl.pallas_call(
+        gram_kernel,
+        in_specs=[
+            pl.BlockSpec(memory_space=pltpu.SMEM),
+            pl.BlockSpec(memory_space=pltpu.VMEM),
+            pl.BlockSpec(memory_space=pl.ANY),
+        ],
+        out_specs=[
+            pl.BlockSpec(memory_space=pltpu.VMEM),
+            pl.BlockSpec(memory_space=pl.ANY),
+        ],
+        out_shape=[
+            jax.ShapeDtypeStruct((peers, height + 1, 1, width), jnp.float32),
+            jax.ShapeDtypeStruct(states.shape, jnp.float32),
+        ],
+        input_output_aliases={2: 1},
+        scratch_shapes=[pltpu.VMEM((width, width), jnp.float32)],
+    )(piece.reshape(1), arrived, states)
+
+
+def total_kernel(parts_ref, piece_ref, project_ref, work):
+    count, rows = parts_ref.shape[:2]
+    for r in range(rows):
+        row = parts_ref[0, r]
+        for i in range(1, count):
+            row = row + parts_ref[i, r]
+        if r < rows - 1:
+            work[r : r + 1, :] = row
+        else:
+            project_ref[...] = row
+    piece = work[...]
+    for i in range(piece_ref.shape[0]):
+        piece_ref[i] = piece
+
+
+def total(parts, peers):
+    rows, width = parts.shape[1] - 1, parts.shape[3]
+    return pl.pallas_call(
+        total_kernel,
+        out_shape=[
+            jax.ShapeDtypeStruct((peers, rows, width), jnp.float32),
+            jax.ShapeDtypeStruct((1, width), jnp.float32),
+        ],
+        scratch_shapes=[pltpu.VMEM((rows, width), jnp.float32)],
+    )(parts)
 
 
 def weights_kernel(mem_ref, gram_ref, project_ref, out_ref, work):
@@ -191,73 +394,31 @@
 
 def on_device(member_heat_solute, velocity, phase_mask, obs_index, obs_value, obs_error):
     members, _, depth, width = member_heat_solute.shape
-    mushy = phase_mask.astype(jnp.float32)
+    pair = member_heat_solute.reshape(members * 2 * depth, width)
+    speed = velocity.reshape(members * depth, width)
     count = lax.axis_size(SPACE)
     position = lax.axis_index(SPACE)
-
-    def edge(first):
-        rows = slice(first, first + 2)
-        return jnp.concatenate(
-            [
-                member_heat_solute[:, 0, rows],
-                member_heat_solute[:, 1, rows],
-                velocity[:, rows],
-                mushy[None, rows],
-            ],
-            axis=0,
-        )
-
-    above = lax.ppermute(edge(depth - 2), SPACE, [(i, i + 1) for i in range(count - 1)])
-    below = lax.ppermute(edge(0), SPACE, [(i + 1, i) for i in range(count - 1)])
-    fields = jnp.concatenate(
-        [member_heat_solute[:, 0], member_heat_solute[:, 1], velocity, mushy[None]], axis=0
+    ends = jnp.stack([position == 0, position == count - 1]).astype(jnp.int32)
+    tail, head = edges(pair, speed, phase_mask)
+    above = lax.ppermute(tail, SPACE, [(i, i + 1) for i in range(count - 1)])
+    below = lax.ppermute(head, SPACE, [(i + 1, i) for i in range(count - 1)])
+    group = ("y", "core", "mem")
+    states, message = forecast(
+        ends, obs_index, obs_value, obs_error, pair, speed, phase_mask, above, below,
+        lax.axis_size(group),
     )
-    padded = jnp.concatenate([above, fields, below], axis=1)
-    mushy = padded[3 * members]
-    factor = 1.0 - mushy * (1.0 - mushy_ratio)
-    heat = padded[:members]
-    solute = padded[members : 2 * members]
-    speed = padded[2 * members : 3 * members]
-    heat, solute, speed = advance(heat, solute, speed, mushy, factor)
-    row = lax.broadcasted_iota(jnp.int32, (depth + 2, 1), 0)
-    outside = ((row == 0) & (position == 0)) | ((row == depth + 1) & (position == count - 1))
-    heat = jnp.where(outside, 0.0, heat)
-    solute = jnp.where(outside, 0.0, solute)
-    speed = jnp.where(outside, 0.0, speed)
-    heat, solute, speed = advance(heat, solute, speed, mushy[1:-1], factor[1:-1])
-
-    temp = heat * factor[2:-2]
-    flat_temp = temp.reshape(members, -1)
-    cell_ids = jnp.arange(flat_temp.shape[1], dtype=jnp.int32)
-    selector = jnp.where(obs_index[:, None] == cell_ids[None, :], 1.0, 0.0).astype(jnp.float32)
-    observed_own = jnp.dot(selector, flat_temp.T, precision=HIGHEST)
-    message = jnp.concatenate([observed_own, obs_value[:, None], obs_error[:, None]], axis=1)
-    arrived = shared(message, ("y", "core", "mem"))
+    arrived = lax.all_to_all(message, group, 0, 0)
+    arrived = arrived.reshape(-1, width)
     mem_size = lax.axis_size("mem")
-    slabs = arrived.shape[0] // mem_size
-    n_obs = message.shape[0]
-    arrived = arrived.reshape(slabs, mem_size, n_obs, members + 2)
-    ensemble = mem_size * members
-    measured = arrived[..., :members].transpose(0, 2, 1, 3).reshape(slabs * n_obs, ensemble)
-    value = arrived[:, 0, :, members].reshape(slabs * n_obs)
-    error = arrived[:, 0, :, members + 1].reshape(slabs * n_obs)
-    mean_obs = jnp.mean(measured, axis=1)
-    spread = (measured - mean_obs[:, None]) / (
-        error[:, None] * jnp.sqrt(jnp.float32(ensemble - 1))
+    pieces = lax.axis_size(("y", "core"))
+    part, states = gram_part(
+        lax.axis_index(("y", "core")), arrived, states, lax.axis_size("z"), mem_size * members // pieces
     )
-    innovation = (value - mean_obs) / error
-    pieces = lax.axis_size(("y", "core"))
-    piece = lax.axis_index(("y", "core"))
-    height = ensemble // pieces
-    own_cols = lax.dynamic_slice_in_dim(spread, piece * height, height, 1)
-    left = jnp.concatenate([own_cols, innovation[:, None]], axis=1)
-    part = lax.dot_general(left, spread, (((0,), (0,)), ((), ())), precision=HIGHEST)
-    part = jnp.sum(shared(part, "z"), axis=0)
-    project = part[height:]
-    gram = shared(part[:height], ("y", "core"))
+    part = lax.all_to_all(part, "z", 0, 0)
+    piece, project = total(part, pieces)
+    gram = lax.all_to_all(piece, ("y", "core"), 0, 0)
     mem_index = lax.axis_index("mem")
     weights = analysis_weights(mem_index, gram, project, members)
-    states = jnp.stack([heat, solute, speed], axis=0).transpose(0, 2, 1, 3)
     sources = [states]
     for step in range(1, mem_size):
         pairs = [((i + step) % mem_size, i) for i in range(mem_size)]

time: 111 us -> 105 us (0.946)
  blocking collectives: 26.8 us -> 43 us
  local copies, waits for them, and re-layouts: 17 us -> 3.38 us
  starting transfers between devices: 42.6 us -> 33.5 us
  Pallas kernels: 7.49 us -> 15.2 us
  other arithmetic: 6.12 us -> 0.08 us
    all_to_all x1 -> x2, blocking collectives: 26.8 us -> 43 us  [the longest x1 28.6 us: on_device(): part = lax.all_to_all(part, 'z', 0, 0)]
    all_to_all x2 -> x1, starting transfers between devices: 15.2 us -> 7.3 us  [on_device(): gram = lax.all_to_all(piece, ('y', 'core'), 0, 0)]
    pallas_call x0 -> x4, Pallas kernels: none -> 7.7 us  [the longest x1 2.1 us: gram_part(): pl.pallas_call(gram_kernel, in_specs=[pl.BlockSpec(memory_space=pltpu.SME...]
    slice x20 -> x0, local copies, waits for them, and re-layouts: 4.41 us -> none  [the longest x6 1.63 us: lateral(): right = jnp.concatenate([field[..., 1:], field[..., -1:]], axis=-1)]
    transpose x2 -> x0, local copies, waits for them, and re-layouts: 4.01 us -> none  [on_device(): arrived[..., :members].transpose(0, 2, 1, 3)]
    unnamed x27 -> x20, local copies, waits for them, and re-layouts: 5.23 us -> 3.38 us
    another operation x1 -> x0, other arithmetic: 1.49 us -> none  [on_device(): states = jnp.stack([heat, solute, speed], axis=0).transpose(0, 2, 1, 3)]
    reshape x1 -> x0, local copies, waits for them, and re-layouts: 1.29 us -> none  [on_device(): arrived[..., :members].transpose(0, 2, 1, 3)]
  transfers between devices with their start and end apart: 7 -> 6, of which waited for: 2 -> 2; matrix products, arithmetic and copies ran while one was open for 11% -> 0% of each run, Pallas kernels for 5% -> 7%
where the time goes in v3:
time: 105 us
  blocking collectives  43 us (41%)
  starting transfers between devices  33.5 us (32%)
  Pallas kernels  15.2 us (14%)
  waiting for transfers between devices  8.85 us (8%)
  local copies, waits for them, and re-layouts  3.38 us (3%)
    all_to_all x1, blocking collectives, on_device(): part = lax.all_to_all(part, 'z', 0, 0)  28.6 us
    all_to_all x1, blocking collectives, on_device(): arrived = lax.all_to_all(message, group, 0, 0)  14.4 us
    ppermute x1, starting transfers between devices, on_device(): below = lax.ppermute(head, SPACE, [(i + 1, i) for i in range(count - 1)])  12.8 us
    ppermute x3, starting transfers between devices, on_device(): sources.append(lax.ppermute(states, 'mem', pairs))  8.86 us
    all_to_all x1, waiting for transfers between devices, on_device(): gram = lax.all_to_all(piece, ('y', 'core'), 0, 0)  7.84 us
    all_to_all x1, starting transfers between devices, on_device(): gram = lax.all_to_all(piece, ('y', 'core'), 0, 0)  7.3 us
    pallas_call x1, Pallas kernels, analysis_weights(): pl.pallas_call(weights_kernel, out_shape=jax.ShapeDtypeStruct((own, membe...  5.55 us
    ppermute x1, starting transfers between devices, on_device(): above = lax.ppermute(tail, SPACE, [(i, i + 1) for i in range(count - 1)])  4.58 us
  transfers between devices with their start and end apart: 6, of which 2 were waited for; matrix products, arithmetic and copies ran while one was open for 0% of the time, Pallas kernels for 7%

profile of v3, /device:TPU:1, one launch (start us, length us, event | category | flops | bytes accessed | tf_op | source)
XLA Modules:
  0.0 104.8 jit_solution(8437458363051271522)
XLA Ops:
  0.6 0.0 copy-start.2
  0.6 0.0 copy-start.3
  0.6 1.9 %shard_map.77 = (f32[200,128]{1,0:T(8,128)}, f32[200,128]{1,0:T(8,128)}) custom-call(f32[1024,128]{1,0:T(8,128)} %bitcast.7, f32[512,128]{1,0:T(8,128)} %bitcast.9, s32[16,128]{1,0:T(8,128)} %mask_ref.3), custom_call_target="tpu_custom_call" | custom-call | tf_op jit(solution)/shard_map/pallas_call | solution.py:65
  2.6 4.6 %collective-permute-start = (f32[200,128]{1,0:T(8,128)}, f32[200,128]{1,0:T(8,128)S(1)}, u32[]{:S(2)}, u32[]{:S(2)}) collective-permute-start(f32[200,128]{1,0:T(8,128)} %get-tuple-element.10), channel_id=1, source_target_pairs={{0,4},{4,8},{8,12},{12,16},{16,20},{20,24},{24,28},{28,32},{32,36}... | collective-permute-start | bytes 307208 | tf_op jit(solution)/shard_map/ppermute | solution.py:403
  7.2 12.8 %collective-permute-start.1 = (f32[200,128]{1,0:T(8,128)}, f32[200,128]{1,0:T(8,128)S(1)}, u32[]{:S(2)}, u32[]{:S(2)}) collective-permute-start(f32[200,128]{1,0:T(8,128)} %get-tuple-element.11), channel_id=1, source_target_pairs={{4,0},{8,4},{12,8},{16,12},{20,16},{24,20},{28,24},{32,28},{36,32}... | collective-permute-start | bytes 307208 | tf_op jit(solution)/shard_map/ppermute | solution.py:404
  20.0 0.0 copy-start.5
  20.0 0.0 copy-start.6
  20.0 0.0 copy-start.7
  20.0 0.0 copy-start.8
  20.0 0.1 add_convert_fusion.ends_ref
  20.1 0.0 collective-permute-done.above_ref
  20.1 1.0 collective-permute-done.1.below_ref
  21.1 0.0 copy-done.3
  21.1 2.1 %shard_map.78 = (f32[3,16,32,128]{3,2,1,0:T(8,128)S(1)}, f32[64,4,128]{2,1,0:T(4,128)S(1)}) custom-call(s32[2]{0:T(128)S(1)} %add_convert_fusion.ends_ref, s32[16]{0:T(128)S(1)} %copy-done.6, f32[16]{0:T(128)S(1)} %copy-done.7, f32[16]{0:T(128)S(1)} %copy-done.8, f32[1024,128]{1,0:T(8,128)S(1)} %bitcast.8, f32[512,128]{1,0:T(8,128)S(1)} %bitcast.10, ...), custom_call_target="tpu_custom_call" | custom-call | tf_op jit(solution)/shard_map/pallas_call | solution.py:166
  23.2 0.9 copy-done
  24.1 14.4 %all_to_all.15 = f32[64,4,128]{2,1,0:T(4,128)} all-to-all(f32[64,4,128]{2,1,0:T(4,128)S(1)} %get-tuple-element.12), channel_id=1, replica_groups=mesh['z'=16,'y'=8,'core'=2,'mem'=4] {'y','core','mem'}, dimensions={0} | all-to-all | bytes 262144 | tf_op jit(solution)/shard_map/all_to_all | solution.py:410
  38.5 2.1 %shard_map.79 = (f32[16,9,1,128]{3,2,1,0:T(1,128)}, f32[3,16,32,128]{3,2,1,0:T(8,128)}) custom-call(s32[1]{0:T(128)} %bitcast.1.piece_ref, f32[256,128]{1,0:T(8,128)} %bitcast.11, f32[3,16,32,128]{3,2,1,0:T(8,128)} %copy-done), custom_call_target="tpu_custom_call", output_to_operand_aliasing={{1}: (2, {})} | custom-call | tf_op jit(solution)/shard_map/pallas_call | solution.py:219
  40.6 2.2 %collective-permute-start.4 = (f32[3,16,32,128]{3,2,1,0:T(8,128)}, f32[3,16,32,128]{3,2,1,0:T(8,128)S(1)}, u32[]{:S(2)}, u32[]{:S(2)}) collective-permute-start(f32[3,16,32,128]{3,2,1,0:T(8,128)} %get-tuple-element.17.refs_0_), channel_id=1, source_target_pairs={{3,0},{0,1},{1,2},{2,3},{7,4},{4,5},{5,6},{6,7},{11,8},{8,9},{9,10... | collective-permute-start | bytes 2359304 | tf_op jit(solution)/shard_map/ppermute | solution.py:425
  42.7 4.2 %collective-permute-start.3 = (f32[3,16,32,128]{3,2,1,0:T(8,128)}, f32[3,16,32,128]{3,2,1,0:T(8,128)S(1)}, u32[]{:S(2)}, u32[]{:S(2)}) collective-permute-start(f32[3,16,32,128]{3,2,1,0:T(8,128)} %get-tuple-element.17.refs_0_), channel_id=1, source_target_pairs={{2,0},{3,1},{0,2},{1,3},{6,4},{7,5},{4,6},{5,7},{10,8},{11,9},{8,1... | collective-permute-start | bytes 2359304 | tf_op jit(solution)/shard_map/ppermute | solution.py:425
  46.9 2.5 %collective-permute-start.2 = (f32[3,16,32,128]{3,2,1,0:T(8,128)}, f32[3,16,32,128]{3,2,1,0:T(8,128)S(1)}, u32[]{:S(2)}, u32[]{:S(2)}) collective-permute-start(f32[3,16,32,128]{3,2,1,0:T(8,128)} %get-tuple-element.17.refs_0_), channel_id=1, source_target_pairs={{1,0},{2,1},{3,2},{0,3},{5,4},{6,5},{7,6},{4,7},{9,8},{10,9},{11,1... | collective-permute-start | bytes 2359304 | tf_op jit(solution)/shard_map/ppermute | solution.py:425
  49.5 28.6 %all_to_all.16.parts_ref = f32[16,9,1,128]{3,2,1,0:T(1,128)} all-to-all(f32[16,9,1,128]{3,2,1,0:T(1,128)} %get-tuple-element.14), channel_id=1, replica_groups=mesh['z'=16,'y'=8,'core'=2,'mem'=4] {'z'}, dimensions={0} | all-to-all | bytes 147456 | tf_op jit(solution)/shard_map/all_to_all | solution.py:417
  78.1 1.6 %shard_map.80 = (f32[16,8,128]{2,1,0:T(8,128)}, f32[1,128]{1,0:T(1,128)}) custom-call(f32[16,9,1,128]{3,2,1,0:T(1,128)} %all_to_all.16.parts_ref), custom_call_target="tpu_custom_call" | custom-call | tf_op jit(solution)/shard_map/pallas_call | solution.py:256
  79.7 7.3 %all-to-all-start.2 = ((f32[16,8,128]{2,1,0:T(8,128)}), f32[16,8,128]{2,1,0:T(8,128)S(1)}, u32[]{:S(2)}, u32[]{:S(2)}) async-start(f32[16,8,128]{2,1,0:T(8,128)} %get-tuple-element.15), calls=%async_computation.2 | async-start | bytes 131072 | tf_op jit(solution)/shard_map/all_to_all | solution.py:419
  87.0 7.8 %all-to-all-done.2.gram_ref = f32[16,8,128]{2,1,0:T(8,128)S(1)} async-done(((f32[16,8,128]{2,1,0:T(8,128)}), f32[16,8,128]{2,1,0:T(8,128)S(1)}, u32[]{:S(2)}, u32[]{:S(2)}) %all-to-all-start.2) | async-done | bytes 65568 | tf_op jit(solution)/shard_map/all_to_all | solution.py:419
  94.8 0.6 copy-done.9
  95.4 5.5 %shard_map.81.weights_ref = f32[32,128]{1,0:T(8,128)} custom-call(s32[1]{0:T(128)} %bitcast.mem_ref, f32[16,8,128]{2,1,0:T(8,128)} %copy-done.9, f32[1,128]{1,0:T(1,128)} %get-tuple-element.16.project_ref), custom_call_target="tpu_custom_call" | custom-call | tf_op jit(solution)/shard_map/pallas_call | solution.py:329
  101.0 0.0 collective-permute-done.4.refs_3_
  101.0 0.0 collective-permute-done.3.refs_2_
  101.0 0.0 collective-permute-done.2.refs_1_
  101.0 1.1 %copy-done.1 = f32[3,16,32,128]{3,2,1,0:T(8,128)S(1)} copy-done((f32[3,16,32,128]{3,2,1,0:T(8,128)S(1)}, f32[3,16,32,128]{3,2,1,0:T(8,128)}, u32[]{:S(2)}) %copy-start.1) | copy-done | bytes 786456
  102.1 0.7 copy-done.4
  102.8 1.9 %shard_map.82 = (f32[32,2,16,128]{3,2,1,0:T(8,128)}, f32[32,16,128]{2,1,0:T(8,128)}) custom-call(f32[32,128]{1,0:T(8,128)S(1)} %copy-done.4, f32[3,16,32,128]{3,2,1,0:T(8,128)S(1)} %copy-done.1, f32[3,16,32,128]{3,2,1,0:T(8,128)S(1)} %collective-permute-done.2.refs_1_, f32[3,16,32,128]{3,2,1,0:T(8,128)S(1)} %collective-permute-done.3.refs_2_, ...), custom_call_target="tpu_custom_call" | custom-call | tf_op jit(solution)/shard_map/pallas_call | solution.py:376
  (9 shorter events, 0.0 us)
Async XLA Ops:
  0.6 20.5 %copy-start.2 = (f32[32,2,16,128]{3,2,1,0:T(8,128)S(1)}, f32[32,2,16,128]{3,2,1,0:T(8,128)}, u32[]{:S(2)}) copy-start(f32[32,2,16,128]{3,2,1,0:T(8,128)} %param.6) | copy-start | bytes 1572868
  0.6 20.5 %copy-start.3 = (f32[32,16,128]{2,1,0:T(8,128)S(1)}, f32[32,16,128]{2,1,0:T(8,128)}, u32[]{:S(2)}) copy-start(f32[32,16,128]{2,1,0:T(8,128)} %param.7) | copy-start | bytes 786436
  2.6 17.5 %collective-permute-start = (f32[200,128]{1,0:T(8,128)}, f32[200,128]{1,0:T(8,128)S(1)}, u32[]{:S(2)}, u32[]{:S(2)}) collective-permute-start(f32[200,128]{1,0:T(8,128)} %get-tuple-element.10), channel_id=1, source_target_pairs={{0,4},{4,8},{8,12},{12,16},{16,20},{20,24},{24,28},{28,32},{32,36}... | collective-permute-start | bytes 307208 | tf_op jit(solution)/shard_map/ppermute | solution.py:403
  7.2 13.9 %collective-permute-start.1 = (f32[200,128]{1,0:T(8,128)}, f32[200,128]{1,0:T(8,128)S(1)}, u32[]{:S(2)}, u32[]{:S(2)}) collective-permute-start(f32[200,128]{1,0:T(8,128)} %get-tuple-element.11), channel_id=1, source_target_pairs={{4,0},{8,4},{12,8},{16,12},{20,16},{24,20},{28,24},{32,28},{36,32}... | collective-permute-start | bytes 307208 | tf_op jit(solution)/shard_map/ppermute | solution.py:404
  20.0 1.1 %copy-start.5 = (s32[16,128]{1,0:T(8,128)S(1)}, s32[16,128]{1,0:T(8,128)}, u32[]{:S(2)}) copy-start(s32[16,128]{1,0:T(8,128)} %mask_ref.3) | copy-start | bytes 24580
  20.0 1.1 %copy-start.6 = (s32[16]{0:T(128)S(1)}, s32[16]{0:T(128)}, u32[]{:S(2)}) copy-start(s32[16]{0:T(128)} %index_ref.1) | copy-start | bytes 196
  20.0 1.1 %copy-start.7 = (f32[16]{0:T(128)S(1)}, f32[16]{0:T(128)}, u32[]{:S(2)}) copy-start(f32[16]{0:T(128)} %value_ref.1) | copy-start | bytes 196
  20.0 1.1 %copy-start.8 = (f32[16]{0:T(128)S(1)}, f32[16]{0:T(128)}, u32[]{:S(2)}) copy-start(f32[16]{0:T(128)} %error_ref.1) | copy-start | bytes 196
  23.2 0.9 copy-start
  40.6 60.4 %collective-permute-start.4 = (f32[3,16,32,128]{3,2,1,0:T(8,128)}, f32[3,16,32,128]{3,2,1,0:T(8,128)S(1)}, u32[]{:S(2)}, u32[]{:S(2)}) collective-permute-start(f32[3,16,32,128]{3,2,1,0:T(8,128)} %get-tuple-element.17.refs_0_), channel_id=1, source_target_pairs={{3,0},{0,1},{1,2},{2,3},{7,4},{4,5},{5,6},{6,7},{11,8},{8,9},{9,10... | collective-permute-start | bytes 2359304 | tf_op jit(solution)/shard_map/ppermute | solution.py:425
  42.7 58.2 %collective-permute-start.3 = (f32[3,16,32,128]{3,2,1,0:T(8,128)}, f32[3,16,32,128]{3,2,1,0:T(8,128)S(1)}, u32[]{:S(2)}, u32[]{:S(2)}) collective-permute-start(f32[3,16,32,128]{3,2,1,0:T(8,128)} %get-tuple-element.17.refs_0_), channel_id=1, source_target_pairs={{2,0},{3,1},{0,2},{1,3},{6,4},{7,5},{4,6},{5,7},{10,8},{11,9},{8,1... | collective-permute-start | bytes 2359304 | tf_op jit(solution)/shard_map/ppermute | solution.py:425
  46.9 54.1 %collective-permute-start.2 = (f32[3,16,32,128]{3,2,1,0:T(8,128)}, f32[3,16,32,128]{3,2,1,0:T(8,128)S(1)}, u32[]{:S(2)}, u32[]{:S(2)}) collective-permute-start(f32[3,16,32,128]{3,2,1,0:T(8,128)} %get-tuple-element.17.refs_0_), channel_id=1, source_target_pairs={{1,0},{2,1},{3,2},{0,3},{5,4},{6,5},{7,6},{4,7},{9,8},{10,9},{11,1... | collective-permute-start | bytes 2359304 | tf_op jit(solution)/shard_map/ppermute | solution.py:425
  79.7 15.1 %all-to-all-start.2 = ((f32[16,8,128]{2,1,0:T(8,128)}), f32[16,8,128]{2,1,0:T(8,128)S(1)}, u32[]{:S(2)}, u32[]{:S(2)}) async-start(f32[16,8,128]{2,1,0:T(8,128)} %get-tuple-element.15), calls=%async_computation.2 | async-start | bytes 131072 | tf_op jit(solution)/shard_map/all_to_all | solution.py:419
  94.8 0.6 copy-start.9
  101.0 1.1 %copy-start.1 = (f32[3,16,32,128]{3,2,1,0:T(8,128)S(1)}, f32[3,16,32,128]{3,2,1,0:T(8,128)}, u32[]{:S(2)}) copy-start(f32[3,16,32,128]{3,2,1,0:T(8,128)} %get-tuple-element.17.refs_0_) | copy-start | bytes 2359300
  102.1 0.7 copy-start.4

commit v4 on v3

--- a/solution.py
+++ b/solution.py
@@ -179,8 +179,7 @@
     )(ends, obs_index, obs_value, obs_error, pair, speed, mask, above, below)
 
 
-def gram_kernel(piece_ref, arrived_ref, states_ref, out_ref, passed_ref, work):
-    del states_ref, passed_ref
+def gram_kernel(piece_ref, arrived_ref, out_ref, work):
     total, width = arrived_ref.shape
     slabs = total // 16
     share = width // 4
@@ -214,26 +213,21 @@
         out_ref[i, height] = project
 
 
-def gram_part(piece, arrived, states, peers, height):
+def gram_part(piece, arrived, peers, height):
     width = arrived.shape[1]
     return pl.pallas_call(
         gram_kernel,
         in_specs=[
             pl.BlockSpec(memory_space=pltpu.SMEM),
             pl.BlockSpec(memory_space=pltpu.VMEM),
-            pl.BlockSpec(memory_space=pl.ANY),
-        ],
-        out_specs=[
-            pl.BlockSpec(memory_space=pltpu.VMEM),
-            pl.BlockSpec(memory_space=pl.ANY),
-        ],
-        out_shape=[
-            jax.ShapeDtypeStruct((peers, height + 1, 1, width), jnp.float32),
-            jax.ShapeDtypeStruct(states.shape, jnp.float32),
-        ],
-        input_output_aliases={2: 1},
+        ],
+        out_specs=pl.BlockSpec(memory_space=pltpu.VMEM),
+        out_shape=jax.ShapeDtypeStruct((peers, height + 1, 1, width), jnp.float32),
         scratch_shapes=[pltpu.VMEM((width, width), jnp.float32)],
-    )(piece.reshape(1), arrived, states)
+        cost_estimate=pl.CostEstimate(
+            flops=10_000_000_000, bytes_accessed=1_000_000, transcendentals=0
+        ),
+    )(piece.reshape(1), arrived)
 
 
 def total_kernel(parts_ref, piece_ref, project_ref, work):
@@ -411,8 +405,8 @@
     arrived = arrived.reshape(-1, width)
     mem_size = lax.axis_size("mem")
     pieces = lax.axis_size(("y", "core"))
-    part, states = gram_part(
-        lax.axis_index(("y", "core")), arrived, states, lax.axis_size("z"), mem_size * members // pieces
+    part = gram_part(
+        lax.axis_index(("y", "core")), arrived, lax.axis_size("z"), mem_size * members // pieces
     )
     part = lax.all_to_all(part, "z", 0, 0)
     piece, project = total(part, pieces)

time: 105 us -> 98.8 us (0.941)
  blocking collectives: 43 us -> 28.7 us
  starting transfers between devices: 33.5 us -> 41.9 us
  local copies, waits for them, and re-layouts: 3.38 us -> 2.03 us
    all_to_all x1 -> x0, blocking collectives: 14.4 us -> none  [on_device(): arrived = lax.all_to_all(message, group, 0, 0)]
    all_to_all x0 -> x1, starting transfers between devices: none -> 4.44 us  [on_device(): arrived = lax.all_to_all(message, group, 0, 0)]
    all_to_all x1, starting transfers between devices: 7.3 us -> 9.43 us  [on_device(): gram = lax.all_to_all(piece, ('y', 'core'), 0, 0)]
    ppermute x3, starting transfers between devices: 8.86 us -> 10.7 us  [on_device(): sources.append(lax.ppermute(states, 'mem', pairs))]
    unnamed x20 -> x18, local copies, waits for them, and re-layouts: 3.38 us -> 2.03 us
  transfers between devices with their start and end apart: 6 -> 7, of which waited for: 2 -> 2; matrix products, arithmetic and copies ran while one was open for 0% -> 0% of each run, Pallas kernels for 7% -> 9%
where the time goes in v4:
time: 98.8 us; the launch traced here: 98.1 us
  starting transfers between devices  41.9 us (42%)
  blocking collectives  28.7 us (29%)
  Pallas kernels  15.8 us (16%)
  waiting for transfers between devices  8.82 us (9%)
  local copies, waits for them, and re-layouts  2.03 us (2%)
    all_to_all x1, blocking collectives, on_device(): part = lax.all_to_all(part, 'z', 0, 0)  28.7 us
    ppermute x1, starting transfers between devices, on_device(): below = lax.ppermute(head, SPACE, [(i + 1, i) for i in range(count - 1)])  12.8 us
    ppermute x3, starting transfers between devices, on_device(): sources.append(lax.ppermute(states, 'mem', pairs))  10.7 us
    all_to_all x1, starting transfers between devices, on_device(): gram = lax.all_to_all(piece, ('y', 'core'), 0, 0)  9.43 us
    all_to_all x1, waiting for transfers between devices, on_device(): gram = lax.all_to_all(piece, ('y', 'core'), 0, 0)  7.81 us
    pallas_call x1, Pallas kernels, analysis_weights(): pl.pallas_call(weights_kernel, out_shape=jax.ShapeDtypeStruct((own, membe...  5.55 us
    ppermute x1, starting transfers between devices, on_device(): above = lax.ppermute(tail, SPACE, [(i, i + 1) for i in range(count - 1)])  4.58 us
    all_to_all x1, starting transfers between devices, on_device(): arrived = lax.all_to_all(message, group, 0, 0)  4.44 us
  transfers between devices with their start and end apart: 7, of which 2 were waited for; matrix products, arithmetic and copies ran while one was open for 0% of the time, Pallas kernels for 9%

profile of v4, /device:TPU:1, one launch (start us, length us, event | category | flops | bytes accessed | tf_op | source)
XLA Modules:
  0.0 98.1 jit_solution(10168083000988765459)
XLA Ops:
  0.6 0.0 copy-start
  0.6 1.9 %shard_map.77 = (f32[200,128]{1,0:T(8,128)}, f32[200,128]{1,0:T(8,128)}) custom-call(f32[1024,128]{1,0:T(8,128)} %bitcast.7, f32[512,128]{1,0:T(8,128)} %bitcast.9, s32[16,128]{1,0:T(8,128)} %mask_ref.3), custom_call_target="tpu_custom_call" | custom-call | tf_op jit(solution)/shard_map/pallas_call | solution.py:65
  2.6 4.6 %collective-permute-start = (f32[200,128]{1,0:T(8,128)}, f32[200,128]{1,0:T(8,128)S(1)}, u32[]{:S(2)}, u32[]{:S(2)}) collective-permute-start(f32[200,128]{1,0:T(8,128)} %get-tuple-element.8), channel_id=1, source_target_pairs={{0,4},{4,8},{8,12},{12,16},{16,20},{20,24},{24,28},{28,32},{32,36}... | collective-permute-start | bytes 307208 | tf_op jit(solution)/shard_map/ppermute | solution.py:397
  7.2 12.8 %collective-permute-start.1 = (f32[200,128]{1,0:T(8,128)}, f32[200,128]{1,0:T(8,128)S(1)}, u32[]{:S(2)}, u32[]{:S(2)}) collective-permute-start(f32[200,128]{1,0:T(8,128)} %get-tuple-element.9), channel_id=1, source_target_pairs={{4,0},{8,4},{12,8},{16,12},{20,16},{24,20},{28,24},{32,28},{36,32}... | collective-permute-start | bytes 307208 | tf_op jit(solution)/shard_map/ppermute | solution.py:398
  20.0 0.0 copy-start.3
  20.0 0.0 copy-start.4
  20.0 0.0 copy-start.5
  20.0 0.0 copy-start.6
  20.0 0.1 add_convert_fusion.ends_ref
  20.1 0.0 collective-permute-done.above_ref
  20.1 1.0 %collective-permute-done.1.below_ref = f32[200,128]{1,0:T(8,128)S(1)} collective-permute-done((f32[200,128]{1,0:T(8,128)}, f32[200,128]{1,0:T(8,128)S(1)}, u32[]{:S(2)}, u32[]{:S(2)}) %collective-permute-start.1) | collective-permute-done | bytes 102432 | tf_op jit(solution)/shard_map/ppermute | solution.py:398
  21.1 2.8 %shard_map.78 = (f32[3,16,32,128]{3,2,1,0:T(8,128)S(1)}, f32[64,4,128]{2,1,0:T(4,128)}) custom-call(s32[2]{0:T(128)S(1)} %add_convert_fusion.ends_ref, s32[16]{0:T(128)S(1)} %copy-done.4, f32[16]{0:T(128)S(1)} %copy-done.5, f32[16]{0:T(128)S(1)} %copy-done.6, f32[1024,128]{1,0:T(8,128)S(1)} %bitcast.8, f32[512,128]{1,0:T(8,128)S(1)} %bitcast.10, ...), custom_call_target="tpu_custom_call" | custom-call | tf_op jit(solution)/shard_map/pallas_call | solution.py:166
  23.9 4.4 %all-to-all-start = ((f32[64,4,128]{2,1,0:T(4,128)}), f32[64,4,128]{2,1,0:T(4,128)S(1)}, u32[]{:S(2)}, u32[]{:S(2)}) async-start(f32[64,4,128]{2,1,0:T(4,128)} %get-tuple-element.10), calls=%async_computation | async-start | bytes 262144 | tf_op jit(solution)/shard_map/all_to_all | solution.py:404
  28.3 3.3 %collective-permute-start.4 = (f32[3,16,32,128]{3,2,1,0:T(8,128)S(1)}, f32[3,16,32,128]{3,2,1,0:T(8,128)S(1)}, u32[]{:S(2)}, u32[]{:S(2)}) collective-permute-start(f32[3,16,32,128]{3,2,1,0:T(8,128)S(1)} %get-tuple-element.13.refs_0_), channel_id=1, source_target_pairs={{3,0},{0,1},{1,2},{2,3},{7,4},{4,5},{5,6},{6,7},{11,8},{8,9},{9,10... | collective-permute-start | bytes 2359304 | tf_op jit(solution)/shard_map/ppermute | solution.py:419
  31.6 4.3 %collective-permute-start.3 = (f32[3,16,32,128]{3,2,1,0:T(8,128)S(1)}, f32[3,16,32,128]{3,2,1,0:T(8,128)S(1)}, u32[]{:S(2)}, u32[]{:S(2)}) collective-permute-start(f32[3,16,32,128]{3,2,1,0:T(8,128)S(1)} %get-tuple-element.13.refs_0_), channel_id=1, source_target_pairs={{2,0},{3,1},{0,2},{1,3},{6,4},{7,5},{4,6},{5,7},{10,8},{11,9},{8,1... | collective-permute-start | bytes 2359304 | tf_op jit(solution)/shard_map/ppermute | solution.py:419
  35.9 3.1 %collective-permute-start.2 = (f32[3,16,32,128]{3,2,1,0:T(8,128)S(1)}, f32[3,16,32,128]{3,2,1,0:T(8,128)S(1)}, u32[]{:S(2)}, u32[]{:S(2)}) collective-permute-start(f32[3,16,32,128]{3,2,1,0:T(8,128)S(1)} %get-tuple-element.13.refs_0_), channel_id=1, source_target_pairs={{1,0},{2,1},{3,2},{0,3},{5,4},{6,5},{7,6},{4,7},{9,8},{10,9},{11,1... | collective-permute-start | bytes 2359304 | tf_op jit(solution)/shard_map/ppermute | solution.py:419
  39.0 0.0 all-to-all-done
  39.0 0.0 copy-start.8
  39.1 0.6 copy-done.8
  39.7 2.1 %shard_map.79 = f32[16,9,1,128]{3,2,1,0:T(1,128)} custom-call(s32[1]{0:T(128)} %bitcast.1.piece_ref, f32[256,128]{1,0:T(8,128)} %bitcast.11), custom_call_target="tpu_custom_call" | custom-call | flops 10000000000 | bytes 1000000 | tf_op jit(solution)/shard_map/pallas_call | solution.py:218
  41.8 28.7 %all_to_all.15.parts_ref = f32[16,9,1,128]{3,2,1,0:T(1,128)} all-to-all(f32[16,9,1,128]{3,2,1,0:T(1,128)} %shard_map.79), channel_id=1, replica_groups=mesh['z'=16,'y'=8,'core'=2,'mem'=4] {'z'}, dimensions={0} | all-to-all | bytes 147456 | tf_op jit(solution)/shard_map/all_to_all | solution.py:411
  70.5 1.6 %shard_map.80 = (f32[16,8,128]{2,1,0:T(8,128)}, f32[1,128]{1,0:T(1,128)}) custom-call(f32[16,9,1,128]{3,2,1,0:T(1,128)} %all_to_all.15.parts_ref), custom_call_target="tpu_custom_call" | custom-call | tf_op jit(solution)/shard_map/pallas_call | solution.py:250
  72.1 9.4 %all-to-all-start.2 = ((f32[16,8,128]{2,1,0:T(8,128)}), f32[16,8,128]{2,1,0:T(8,128)S(1)}, u32[]{:S(2)}, u32[]{:S(2)}) async-start(f32[16,8,128]{2,1,0:T(8,128)} %get-tuple-element.11), calls=%async_computation.2 | async-start | bytes 131072 | tf_op jit(solution)/shard_map/all_to_all | solution.py:413
  81.5 7.8 %all-to-all-done.2.gram_ref = f32[16,8,128]{2,1,0:T(8,128)S(1)} async-done(((f32[16,8,128]{2,1,0:T(8,128)}), f32[16,8,128]{2,1,0:T(8,128)S(1)}, u32[]{:S(2)}, u32[]{:S(2)}) %all-to-all-start.2) | async-done | bytes 65568 | tf_op jit(solution)/shard_map/all_to_all | solution.py:413
  89.3 0.6 copy-done.7
  89.9 5.5 %shard_map.81.weights_ref = f32[32,128]{1,0:T(8,128)} custom-call(s32[1]{0:T(128)} %bitcast.mem_ref, f32[16,8,128]{2,1,0:T(8,128)} %copy-done.7, f32[1,128]{1,0:T(1,128)} %get-tuple-element.12.project_ref), custom_call_target="tpu_custom_call" | custom-call | tf_op jit(solution)/shard_map/pallas_call | solution.py:323
  95.5 0.0 collective-permute-done.4.refs_3_
  95.5 0.0 collective-permute-done.3.refs_2_
  95.5 0.0 collective-permute-done.2.refs_1_
  95.5 0.0 copy-start.2
  95.5 0.7 copy-done.2
  96.2 1.9 %shard_map.82 = (f32[32,2,16,128]{3,2,1,0:T(8,128)}, f32[32,16,128]{2,1,0:T(8,128)}) custom-call(f32[32,128]{1,0:T(8,128)S(1)} %copy-done.2, f32[3,16,32,128]{3,2,1,0:T(8,128)S(1)} %get-tuple-element.13.refs_0_, f32[3,16,32,128]{3,2,1,0:T(8,128)S(1)} %collective-permute-done.2.refs_1_, f32[3,16,32,128]{3,2,1,0:T(8,128)S(1)} %collective-permute-done.3.refs_2_, ...), custom_call_target="tpu_custom_call" | custom-call | tf_op jit(solution)/shard_map/pallas_call | solution.py:370
  (8 shorter events, 0.0 us)
Async XLA Ops:
  0.6 20.5 %copy-start = (f32[32,2,16,128]{3,2,1,0:T(8,128)S(1)}, f32[32,2,16,128]{3,2,1,0:T(8,128)}, u32[]{:S(2)}) copy-start(f32[32,2,16,128]{3,2,1,0:T(8,128)} %param.6) | copy-start | bytes 1572868
  0.6 20.5 %copy-start.1 = (f32[32,16,128]{2,1,0:T(8,128)S(1)}, f32[32,16,128]{2,1,0:T(8,128)}, u32[]{:S(2)}) copy-start(f32[32,16,128]{2,1,0:T(8,128)} %param.7) | copy-start | bytes 786436
  2.6 17.5 %collective-permute-start = (f32[200,128]{1,0:T(8,128)}, f32[200,128]{1,0:T(8,128)S(1)}, u32[]{:S(2)}, u32[]{:S(2)}) collective-permute-start(f32[200,128]{1,0:T(8,128)} %get-tuple-element.8), channel_id=1, source_target_pairs={{0,4},{4,8},{8,12},{12,16},{16,20},{20,24},{24,28},{28,32},{32,36}... | collective-permute-start | bytes 307208 | tf_op jit(solution)/shard_map/ppermute | solution.py:397
  7.2 13.9 %collective-permute-start.1 = (f32[200,128]{1,0:T(8,128)}, f32[200,128]{1,0:T(8,128)S(1)}, u32[]{:S(2)}, u32[]{:S(2)}) collective-permute-start(f32[200,128]{1,0:T(8,128)} %get-tuple-element.9), channel_id=1, source_target_pairs={{4,0},{8,4},{12,8},{16,12},{20,16},{24,20},{28,24},{32,28},{36,32}... | collective-permute-start | bytes 307208 | tf_op jit(solution)/shard_map/ppermute | solution.py:398
  20.0 1.1 %copy-start.3 = (s32[16,128]{1,0:T(8,128)S(1)}, s32[16,128]{1,0:T(8,128)}, u32[]{:S(2)}) copy-start(s32[16,128]{1,0:T(8,128)} %mask_ref.3) | copy-start | bytes 24580
  20.0 1.1 %copy-start.4 = (s32[16]{0:T(128)S(1)}, s32[16]{0:T(128)}, u32[]{:S(2)}) copy-start(s32[16]{0:T(128)} %index_ref.1) | copy-start | bytes 196
  20.0 1.1 %copy-start.5 = (f32[16]{0:T(128)S(1)}, f32[16]{0:T(128)}, u32[]{:S(2)}) copy-start(f32[16]{0:T(128)} %value_ref.1) | copy-start | bytes 196
  20.0 1.1 %copy-start.6 = (f32[16]{0:T(128)S(1)}, f32[16]{0:T(128)}, u32[]{:S(2)}) copy-start(f32[16]{0:T(128)} %error_ref.1) | copy-start | bytes 196
  23.9 15.2 %all-to-all-start = ((f32[64,4,128]{2,1,0:T(4,128)}), f32[64,4,128]{2,1,0:T(4,128)S(1)}, u32[]{:S(2)}, u32[]{:S(2)}) async-start(f32[64,4,128]{2,1,0:T(4,128)} %get-tuple-element.10), calls=%async_computation | async-start | bytes 262144 | tf_op jit(solution)/shard_map/all_to_all | solution.py:404
  28.3 67.1 %collective-permute-start.4 = (f32[3,16,32,128]{3,2,1,0:T(8,128)S(1)}, f32[3,16,32,128]{3,2,1,0:T(8,128)S(1)}, u32[]{:S(2)}, u32[]{:S(2)}) collective-permute-start(f32[3,16,32,128]{3,2,1,0:T(8,128)S(1)} %get-tuple-element.13.refs_0_), channel_id=1, source_target_pairs={{3,0},{0,1},{1,2},{2,3},{7,4},{4,5},{5,6},{6,7},{11,8},{8,9},{9,10... | collective-permute-start | bytes 2359304 | tf_op jit(solution)/shard_map/ppermute | solution.py:419
  31.6 63.9 %collective-permute-start.3 = (f32[3,16,32,128]{3,2,1,0:T(8,128)S(1)}, f32[3,16,32,128]{3,2,1,0:T(8,128)S(1)}, u32[]{:S(2)}, u32[]{:S(2)}) collective-permute-start(f32[3,16,32,128]{3,2,1,0:T(8,128)S(1)} %get-tuple-element.13.refs_0_), channel_id=1, source_target_pairs={{2,0},{3,1},{0,2},{1,3},{6,4},{7,5},{4,6},{5,7},{10,8},{11,9},{8,1... | collective-permute-start | bytes 2359304 | tf_op jit(solution)/shard_map/ppermute | solution.py:419
  35.9 59.5 %collective-permute-start.2 = (f32[3,16,32,128]{3,2,1,0:T(8,128)S(1)}, f32[3,16,32,128]{3,2,1,0:T(8,128)S(1)}, u32[]{:S(2)}, u32[]{:S(2)}) collective-permute-start(f32[3,16,32,128]{3,2,1,0:T(8,128)S(1)} %get-tuple-element.13.refs_0_), channel_id=1, source_target_pairs={{1,0},{2,1},{3,2},{0,3},{5,4},{6,5},{7,6},{4,7},{9,8},{10,9},{11,1... | collective-permute-start | bytes 2359304 | tf_op jit(solution)/shard_map/ppermute | solution.py:419
  39.0 0.7 copy-start.8
  72.1 17.2 %all-to-all-start.2 = ((f32[16,8,128]{2,1,0:T(8,128)}), f32[16,8,128]{2,1,0:T(8,128)S(1)}, u32[]{:S(2)}, u32[]{:S(2)}) async-start(f32[16,8,128]{2,1,0:T(8,128)} %get-tuple-element.11), calls=%async_computation.2 | async-start | bytes 131072 | tf_op jit(solution)/shard_map/all_to_all | solution.py:413
  89.3 0.6 copy-start.7
  95.5 0.7 copy-start.2

commit v5 on v4

--- a/solution.py
+++ b/solution.py
@@ -318,21 +318,6 @@
     out_ref[...] = pltpu.roll(work[pl.ds(first, own), :], turn, 1)
 
 
-def analysis_weights(mem_index, gram, project, own):
-    members = gram.shape[2]
-    return pl.pallas_call(
-        weights_kernel,
-        out_shape=jax.ShapeDtypeStruct((own, members), jnp.float32),
-        in_specs=[
-            pl.BlockSpec(memory_space=pltpu.SMEM),
-            pl.BlockSpec(memory_space=pltpu.VMEM),
-            pl.BlockSpec(memory_space=pltpu.VMEM),
-        ],
-        out_specs=pl.BlockSpec(memory_space=pltpu.VMEM),
-        scratch_shapes=[pltpu.VMEM((members, members), jnp.float32)],
-    )(mem_index.reshape(1), gram, project)
-
-
 def mix_kernel(weights_ref, *refs):
     *sources, pair_ref, speed_ref = refs
     kinds, depth, members, width = sources[0].shape
@@ -364,14 +349,27 @@
                     speed_ref[:, row + i, :] = part
 
 
-def mix(weights, sources):
+def analysis_kernel(mem_ref, gram_ref, project_ref, *refs):
+    *blocks, work, weights = refs
+
+    @pl.when(pl.program_id(0) == 0)
+    def _():
+        weights_kernel(mem_ref, gram_ref, project_ref, weights, work)
+
+    mix_kernel(weights, *blocks)
+
+
+def analysis(mem_index, gram, project, sources):
     groups = len(sources)
     kinds, depth, members, width = sources[0].shape
+    ensemble = groups * members
     return pl.pallas_call(
-        mix_kernel,
+        analysis_kernel,
         grid=(2,),
         in_specs=[
-            pl.BlockSpec((members, groups * members), lambda i: (0, 0)),
+            pl.BlockSpec(memory_space=pltpu.SMEM),
+            pl.BlockSpec(gram.shape, lambda i: (0, 0, 0)),
+            pl.BlockSpec(project.shape, lambda i: (0, 0)),
         ]
         + [pl.BlockSpec((kinds, depth // 2, members, width), lambda i: (0, i, 0, 0))] * groups,
         out_specs=[
@@ -382,8 +380,12 @@
             jax.ShapeDtypeStruct((members, 2, depth, width), jnp.float32),
             jax.ShapeDtypeStruct((members, depth, width), jnp.float32),
         ],
+        scratch_shapes=[
+            pltpu.VMEM((ensemble, ensemble), jnp.float32),
+            pltpu.VMEM((members, ensemble), jnp.float32),
+        ],
         compiler_params=pltpu.CompilerParams(vmem_limit_bytes=24 * 1024 * 1024),
-    )(weights, *sources)
+    )(mem_index.reshape(1), gram, project, *sources)
 
 
 def on_device(member_heat_solute, velocity, phase_mask, obs_index, obs_value, obs_error):
@@ -412,12 +414,11 @@
     piece, project = total(part, pieces)
     gram = lax.all_to_all(piece, ("y", "core"), 0, 0)
     mem_index = lax.axis_index("mem")
-    weights = analysis_weights(mem_index, gram, project, members)
     sources = [states]
     for step in range(1, mem_size):
         pairs = [((i + step) % mem_size, i) for i in range(mem_size)]
         sources.append(lax.ppermute(states, "mem", pairs))
-    return mix(weights, sources)
+    return analysis(mem_index, gram, project, sources)
 
 
 def solution(mesh):

time: 98.8 us -> 96.5 us (0.977)
  Pallas kernels: 15.8 us -> 14.4 us
    pallas_call x2 -> x1, Pallas kernels: 7.49 us -> 6 us  [analysis(): pl.pallas_call(analysis_kernel, grid=(2,), in_specs=[pl.BlockSpec(memory_...]
    unnamed x18 -> x16, local copies, waits for them, and re-layouts: 2.03 us -> 1.33 us
  transfers between devices with their start and end apart: 7 -> 7, of which waited for: 2 -> 2; matrix products, arithmetic and copies ran while one was open for 0% -> 0% of each run, Pallas kernels for 9% -> 4%
where the time goes in v5:
time: 96.5 us; the launch traced here: 96 us
  starting transfers between devices  41.9 us (43%)
  blocking collectives  28.7 us (30%)
  Pallas kernels  14.4 us (15%)
  waiting for transfers between devices  8.82 us (9%)
  local copies, waits for them, and re-layouts  1.33 us (1%)
    all_to_all x1, blocking collectives, on_device(): part = lax.all_to_all(part, 'z', 0, 0)  28.7 us
    ppermute x1, starting transfers between devices, on_device(): below = lax.ppermute(head, SPACE, [(i + 1, i) for i in range(count - 1)])  12.8 us
    ppermute x3, starting transfers between devices, on_device(): sources.append(lax.ppermute(states, 'mem', pairs))  10.7 us
    all_to_all x1, starting transfers between devices, on_device(): gram = lax.all_to_all(piece, ('y', 'core'), 0, 0)  9.43 us
    all_to_all x1, waiting for transfers between devices, on_device(): gram = lax.all_to_all(piece, ('y', 'core'), 0, 0)  7.81 us
    pallas_call x1, Pallas kernels, analysis(): pl.pallas_call(analysis_kernel, grid=(2,), in_specs=[pl.BlockSpec(memory_...  6 us
    ppermute x1, starting transfers between devices, on_device(): above = lax.ppermute(tail, SPACE, [(i, i + 1) for i in range(count - 1)])  4.58 us
    all_to_all x1, starting transfers between devices, on_device(): arrived = lax.all_to_all(message, group, 0, 0)  4.44 us
  transfers between devices with their start and end apart: 7, of which 2 were waited for; matrix products, arithmetic and copies ran while one was open for 0% of the time, Pallas kernels for 4%

profile of v5, /device:TPU:1, one launch (start us, length us, event | category | flops | bytes accessed | tf_op | source)
XLA Modules:
  0.0 96.0 jit_solution(3748720283826099944)
XLA Ops:
  0.6 0.0 copy-start
  0.6 0.0 copy-start.1
  0.6 1.9 %shard_map.77 = (f32[200,128]{1,0:T(8,128)}, f32[200,128]{1,0:T(8,128)}) custom-call(f32[1024,128]{1,0:T(8,128)} %bitcast.7, f32[512,128]{1,0:T(8,128)} %bitcast.9, s32[16,128]{1,0:T(8,128)} %mask_ref.3), custom_call_target="tpu_custom_call" | custom-call | tf_op jit(solution)/shard_map/pallas_call | solution.py:65
  2.6 4.6 %collective-permute-start = (f32[200,128]{1,0:T(8,128)}, f32[200,128]{1,0:T(8,128)S(1)}, u32[]{:S(2)}, u32[]{:S(2)}) collective-permute-start(f32[200,128]{1,0:T(8,128)} %get-tuple-element.8), channel_id=1, source_target_pairs={{0,4},{4,8},{8,12},{12,16},{16,20},{20,24},{24,28},{28,32},{32,36}... | collective-permute-start | bytes 307208 | tf_op jit(solution)/shard_map/ppermute | solution.py:399
  7.2 12.8 %collective-permute-start.1 = (f32[200,128]{1,0:T(8,128)}, f32[200,128]{1,0:T(8,128)S(1)}, u32[]{:S(2)}, u32[]{:S(2)}) collective-permute-start(f32[200,128]{1,0:T(8,128)} %get-tuple-element.9), channel_id=1, source_target_pairs={{4,0},{8,4},{12,8},{16,12},{20,16},{24,20},{28,24},{32,28},{36,32}... | collective-permute-start | bytes 307208 | tf_op jit(solution)/shard_map/ppermute | solution.py:400
  20.0 0.0 copy-start.2
  20.0 0.0 copy-start.3
  20.0 0.0 copy-start.4
  20.0 0.0 copy-start.5
  20.0 0.1 add_convert_fusion.ends_ref
  20.1 0.0 collective-permute-done.above_ref
  20.1 1.0 %collective-permute-done.1.below_ref = f32[200,128]{1,0:T(8,128)S(1)} collective-permute-done((f32[200,128]{1,0:T(8,128)}, f32[200,128]{1,0:T(8,128)S(1)}, u32[]{:S(2)}, u32[]{:S(2)}) %collective-permute-start.1) | collective-permute-done | bytes 102432 | tf_op jit(solution)/shard_map/ppermute | solution.py:400
  21.1 0.0 copy-done
  21.1 2.8 %shard_map.78 = (f32[3,16,32,128]{3,2,1,0:T(8,128)S(1)}, f32[64,4,128]{2,1,0:T(4,128)}) custom-call(s32[2]{0:T(128)S(1)} %add_convert_fusion.ends_ref, s32[16]{0:T(128)S(1)} %copy-done.3, f32[16]{0:T(128)S(1)} %copy-done.4, f32[16]{0:T(128)S(1)} %copy-done.5, f32[1024,128]{1,0:T(8,128)S(1)} %bitcast.8, f32[512,128]{1,0:T(8,128)S(1)} %bitcast.10, ...), custom_call_target="tpu_custom_call" | custom-call | tf_op jit(solution)/shard_map/pallas_call | solution.py:166
  23.9 4.4 %all-to-all-start = ((f32[64,4,128]{2,1,0:T(4,128)}), f32[64,4,128]{2,1,0:T(4,128)S(1)}, u32[]{:S(2)}, u32[]{:S(2)}) async-start(f32[64,4,128]{2,1,0:T(4,128)} %get-tuple-element.10), calls=%async_computation | async-start | bytes 262144 | tf_op jit(solution)/shard_map/all_to_all | solution.py:406
  28.3 3.3 %collective-permute-start.4 = (f32[3,16,32,128]{3,2,1,0:T(8,128)S(1)}, f32[3,16,32,128]{3,2,1,0:T(8,128)S(1)}, u32[]{:S(2)}, u32[]{:S(2)}) collective-permute-start(f32[3,16,32,128]{3,2,1,0:T(8,128)S(1)} %get-tuple-element.13.refs_0_), channel_id=1, source_target_pairs={{3,0},{0,1},{1,2},{2,3},{7,4},{4,5},{5,6},{6,7},{11,8},{8,9},{9,10... | collective-permute-start | bytes 2359304 | tf_op jit(solution)/shard_map/ppermute | solution.py:420
  31.6 4.3 %collective-permute-start.3 = (f32[3,16,32,128]{3,2,1,0:T(8,128)S(1)}, f32[3,16,32,128]{3,2,1,0:T(8,128)S(1)}, u32[]{:S(2)}, u32[]{:S(2)}) collective-permute-start(f32[3,16,32,128]{3,2,1,0:T(8,128)S(1)} %get-tuple-element.13.refs_0_), channel_id=1, source_target_pairs={{2,0},{3,1},{0,2},{1,3},{6,4},{7,5},{4,6},{5,7},{10,8},{11,9},{8,1... | collective-permute-start | bytes 2359304 | tf_op jit(solution)/shard_map/ppermute | solution.py:420
  35.9 3.1 %collective-permute-start.2 = (f32[3,16,32,128]{3,2,1,0:T(8,128)S(1)}, f32[3,16,32,128]{3,2,1,0:T(8,128)S(1)}, u32[]{:S(2)}, u32[]{:S(2)}) collective-permute-start(f32[3,16,32,128]{3,2,1,0:T(8,128)S(1)} %get-tuple-element.13.refs_0_), channel_id=1, source_target_pairs={{1,0},{2,1},{3,2},{0,3},{5,4},{6,5},{7,6},{4,7},{9,8},{10,9},{11,1... | collective-permute-start | bytes 2359304 | tf_op jit(solution)/shard_map/ppermute | solution.py:420
  39.0 0.0 all-to-all-done
  39.0 0.0 copy-start.7
  39.1 0.6 copy-done.7
  39.7 2.1 %shard_map.79 = f32[16,9,1,128]{3,2,1,0:T(1,128)} custom-call(s32[1]{0:T(128)} %bitcast.1.piece_ref, f32[256,128]{1,0:T(8,128)} %bitcast.11), custom_call_target="tpu_custom_call" | custom-call | flops 10000000000 | bytes 1000000 | tf_op jit(solution)/shard_map/pallas_call | solution.py:218
  41.8 28.7 %all_to_all.15.parts_ref = f32[16,9,1,128]{3,2,1,0:T(1,128)} all-to-all(f32[16,9,1,128]{3,2,1,0:T(1,128)} %shard_map.79), channel_id=1, replica_groups=mesh['z'=16,'y'=8,'core'=2,'mem'=4] {'z'}, dimensions={0} | all-to-all | bytes 147456 | tf_op jit(solution)/shard_map/all_to_all | solution.py:413
  70.5 1.6 %shard_map.80 = (f32[16,8,128]{2,1,0:T(8,128)}, f32[1,128]{1,0:T(1,128)}) custom-call(f32[16,9,1,128]{3,2,1,0:T(1,128)} %all_to_all.15.parts_ref), custom_call_target="tpu_custom_call" | custom-call | tf_op jit(solution)/shard_map/pallas_call | solution.py:250
  72.1 9.4 %all-to-all-start.2 = ((f32[16,8,128]{2,1,0:T(8,128)}), f32[16,8,128]{2,1,0:T(8,128)S(1)}, u32[]{:S(2)}, u32[]{:S(2)}) async-start(f32[16,8,128]{2,1,0:T(8,128)} %get-tuple-element.11), calls=%async_computation.2 | async-start | bytes 131072 | tf_op jit(solution)/shard_map/all_to_all | solution.py:415
  81.5 7.8 %all-to-all-done.2.gram_ref = f32[16,8,128]{2,1,0:T(8,128)S(1)} async-done(((f32[16,8,128]{2,1,0:T(8,128)}), f32[16,8,128]{2,1,0:T(8,128)S(1)}, u32[]{:S(2)}, u32[]{:S(2)}) %all-to-all-start.2) | async-done | bytes 65568 | tf_op jit(solution)/shard_map/all_to_all | solution.py:415
  89.3 0.0 collective-permute-done.4.refs_3_
  89.3 0.0 collective-permute-done.3.refs_2_
  89.3 0.0 collective-permute-done.2.refs_1_
  89.3 0.0 copy-start.6
  89.3 0.6 copy-done.6
  90.0 6.0 %shard_map.81 = (f32[32,2,16,128]{3,2,1,0:T(8,128)}, f32[32,16,128]{2,1,0:T(8,128)}) custom-call(s32[1]{0:T(128)} %bitcast.mem_ref, f32[16,8,128]{2,1,0:T(8,128)S(1)} %all-to-all-done.2.gram_ref, f32[1,128]{1,0:T(1,128)S(1)} %copy-done.6, f32[3,16,32,128]{3,2,1,0:T(8,128)S(1)} %get-tuple-element.13.refs_0_, ...), custom_call_target="tpu_custom_call" | custom-call | tf_op jit(solution)/shard_map/pallas_call | solution.py:366
  (5 shorter events, 0.0 us)
Async XLA Ops:
  0.6 20.5 %copy-start = (f32[32,2,16,128]{3,2,1,0:T(8,128)S(1)}, f32[32,2,16,128]{3,2,1,0:T(8,128)}, u32[]{:S(2)}) copy-start(f32[32,2,16,128]{3,2,1,0:T(8,128)} %param.6) | copy-start | bytes 1572868
  0.6 20.5 %copy-start.1 = (f32[32,16,128]{2,1,0:T(8,128)S(1)}, f32[32,16,128]{2,1,0:T(8,128)}, u32[]{:S(2)}) copy-start(f32[32,16,128]{2,1,0:T(8,128)} %param.7) | copy-start | bytes 786436
  2.6 17.5 %collective-permute-start = (f32[200,128]{1,0:T(8,128)}, f32[200,128]{1,0:T(8,128)S(1)}, u32[]{:S(2)}, u32[]{:S(2)}) collective-permute-start(f32[200,128]{1,0:T(8,128)} %get-tuple-element.8), channel_id=1, source_target_pairs={{0,4},{4,8},{8,12},{12,16},{16,20},{20,24},{24,28},{28,32},{32,36}... | collective-permute-start | bytes 307208 | tf_op jit(solution)/shard_map/ppermute | solution.py:399
  7.2 13.9 %collective-permute-start.1 = (f32[200,128]{1,0:T(8,128)}, f32[200,128]{1,0:T(8,128)S(1)}, u32[]{:S(2)}, u32[]{:S(2)}) collective-permute-start(f32[200,128]{1,0:T(8,128)} %get-tuple-element.9), channel_id=1, source_target_pairs={{4,0},{8,4},{12,8},{16,12},{20,16},{24,20},{28,24},{32,28},{36,32}... | collective-permute-start | bytes 307208 | tf_op jit(solution)/shard_map/ppermute | solution.py:400
  20.0 1.1 %copy-start.2 = (s32[16,128]{1,0:T(8,128)S(1)}, s32[16,128]{1,0:T(8,128)}, u32[]{:S(2)}) copy-start(s32[16,128]{1,0:T(8,128)} %mask_ref.3) | copy-start | bytes 24580
  20.0 1.1 %copy-start.3 = (s32[16]{0:T(128)S(1)}, s32[16]{0:T(128)}, u32[]{:S(2)}) copy-start(s32[16]{0:T(128)} %index_ref.1) | copy-start | bytes 196
  20.0 1.1 %copy-start.4 = (f32[16]{0:T(128)S(1)}, f32[16]{0:T(128)}, u32[]{:S(2)}) copy-start(f32[16]{0:T(128)} %value_ref.1) | copy-start | bytes 196
  20.0 1.1 %copy-start.5 = (f32[16]{0:T(128)S(1)}, f32[16]{0:T(128)}, u32[]{:S(2)}) copy-start(f32[16]{0:T(128)} %error_ref.1) | copy-start | bytes 196
  23.9 15.2 %all-to-all-start = ((f32[64,4,128]{2,1,0:T(4,128)}), f32[64,4,128]{2,1,0:T(4,128)S(1)}, u32[]{:S(2)}, u32[]{:S(2)}) async-start(f32[64,4,128]{2,1,0:T(4,128)} %get-tuple-element.10), calls=%async_computation | async-start | bytes 262144 | tf_op jit(solution)/shard_map/all_to_all | solution.py:406
  28.3 61.0 %collective-permute-start.4 = (f32[3,16,32,128]{3,2,1,0:T(8,128)S(1)}, f32[3,16,32,128]{3,2,1,0:T(8,128)S(1)}, u32[]{:S(2)}, u32[]{:S(2)}) collective-permute-start(f32[3,16,32,128]{3,2,1,0:T(8,128)S(1)} %get-tuple-element.13.refs_0_), channel_id=1, source_target_pairs={{3,0},{0,1},{1,2},{2,3},{7,4},{4,5},{5,6},{6,7},{11,8},{8,9},{9,10... | collective-permute-start | bytes 2359304 | tf_op jit(solution)/shard_map/ppermute | solution.py:420
  31.6 57.7 %collective-permute-start.3 = (f32[3,16,32,128]{3,2,1,0:T(8,128)S(1)}, f32[3,16,32,128]{3,2,1,0:T(8,128)S(1)}, u32[]{:S(2)}, u32[]{:S(2)}) collective-permute-start(f32[3,16,32,128]{3,2,1,0:T(8,128)S(1)} %get-tuple-element.13.refs_0_), channel_id=1, source_target_pairs={{2,0},{3,1},{0,2},{1,3},{6,4},{7,5},{4,6},{5,7},{10,8},{11,9},{8,1... | collective-permute-start | bytes 2359304 | tf_op jit(solution)/shard_map/ppermute | solution.py:420
  35.9 53.4 %collective-permute-start.2 = (f32[3,16,32,128]{3,2,1,0:T(8,128)S(1)}, f32[3,16,32,128]{3,2,1,0:T(8,128)S(1)}, u32[]{:S(2)}, u32[]{:S(2)}) collective-permute-start(f32[3,16,32,128]{3,2,1,0:T(8,128)S(1)} %get-tuple-element.13.refs_0_), channel_id=1, source_target_pairs={{1,0},{2,1},{3,2},{0,3},{5,4},{6,5},{7,6},{4,7},{9,8},{10,9},{11,1... | collective-permute-start | bytes 2359304 | tf_op jit(solution)/shard_map/ppermute | solution.py:420
  39.0 0.7 copy-start.7
  72.1 17.2 %all-to-all-start.2 = ((f32[16,8,128]{2,1,0:T(8,128)}), f32[16,8,128]{2,1,0:T(8,128)S(1)}, u32[]{:S(2)}, u32[]{:S(2)}) async-start(f32[16,8,128]{2,1,0:T(8,128)} %get-tuple-element.11), calls=%async_computation.2 | async-start | bytes 131072 | tf_op jit(solution)/shard_map/all_to_all | solution.py:415
  89.3 0.7 copy-start.6
